TPU v7x, 32 devices: a whole 2x2x4 slice. The times are simulated.
32 devices in a mesh: dp: 8 (over y, x, core), tensor: 4 (over z).
Axes of the slice: x: 2, y: 2, z: 4, core: 2. Of those that a mesh axis runs over, the one named last changes fastest.
Arguments:
- tokens: bfloat16 [8192, 1024], P(('dp', 'tensor')), may hold values from -6 to 6
- cotangent: bfloat16 [8192, 1024], P(('dp', 'tensor')), may hold values from -6 to 6
- norm_gain: float32 [1024], replicated, may hold values from 0.1 to 1.9
- w_gate: bfloat16 [1024, 2048], P('dp', 'tensor'), may hold values from -0.1875 to 0.1875
- w_value: bfloat16 [1024, 2048], P('dp', 'tensor'), may hold values from -0.1875 to 0.1875
- w_bc: bfloat16 [1024, 256], P('dp'), may hold values from -0.1875 to 0.1875
- w_step: bfloat16 [1024, 32], P('dp', 'tensor'), may hold values from -0.1875 to 0.1875
- conv_value: float32 [5, 2048], P(None, 'tensor'), may hold values from -3 to 3
- conv_bc: float32 [5, 256], replicated, may hold values from -3 to 3
- head_params: float32 [3, 32], P(None, 'tensor'), may hold values from -2 to 1
- gnorm_gain: float32 [2048], P('tensor'), may hold values from 0.1 to 1.9
- w_out: bfloat16 [2048, 1024], P('tensor', 'dp'), may hold values from -0.125 to 0.125
Outputs:
- block_out: float32 [8192, 1024], P(('dp', 'tensor'))
- grad_input: float32 [8192, 1024], P(('dp', 'tensor'))
- grad_norm_gain: float32 [1024], replicated
- grad_w_gate: float32 [1024, 2048], P('dp', 'tensor')
- grad_w_value: float32 [1024, 2048], P('dp', 'tensor')
- grad_w_bc: float32 [1024, 256], P('dp')
- grad_w_step: float32 [1024, 32], P('dp', 'tensor')
- grad_conv_value: float32 [5, 2048], P(None, 'tensor')
- grad_conv_bc: float32 [5, 256], replicated
- grad_head_params: float32 [3, 32], P(None, 'tensor')
- grad_gnorm_gain: float32 [2048], P('tensor')
- grad_w_out: float32 [2048, 1024], P('tensor', 'dp')
All inputs are finite; a program needn't handle non-finite values.
Results may differ from a plain program's by a relative error of at most 0.02.
Values may be sent and summed in bfloat16 or wider, within the bound.
A program may use at most 128 MiB of HBM per device.

v0:
```python
import jax
import jax.numpy as jnp
from jax import lax
from jax.sharding import PartitionSpec as P

D = 1024
HEADS = 32
SPAN = 256
SEQLEN = 1024
INNER = 2048


EPSILON = 1e-05
HIGHEST = lax.Precision.HIGHEST


def causal(sequence, taps):
    width = taps.shape[0] - 1
    padded = jnp.pad(sequence, ((width - 1, 0), (0, 0)))
    total = jnp.zeros_like(sequence) + taps[width]
    for offset in range(width):
        total = total + taps[offset] * padded[offset : offset + sequence.shape[0]]
    return total


def scan_state(values, step_size, rate, b_map, c_map):
    length, heads, hdim_local = values.shape
    count = length // SPAN
    values_c = values.reshape(count, SPAN, heads, hdim_local)
    step_c = step_size.reshape(count, SPAN, heads)
    b_c = b_map.reshape(count, SPAN, b_map.shape[1])
    c_c = c_map.reshape(count, SPAN, c_map.shape[1])
    lower = (
        lax.broadcasted_iota(jnp.int32, (SPAN, SPAN), 0)
        >= lax.broadcasted_iota(jnp.int32, (SPAN, SPAN), 1)
    )[None, :, :]

    def span_step(state, block):
        block_values, block_step, block_b, block_c = block
        logdecay = jnp.cumsum(block_step * rate[None, :], axis=0)
        heads_first = logdecay.T
        inner_prod = jnp.dot(
            block_c, block_b.T, precision=HIGHEST, preferred_element_type=jnp.float32
        )
        spacing = heads_first[:, :, None] - heads_first[:, None, :]
        kernel = jnp.where(lower, jnp.exp(jnp.where(lower, spacing, -60.0)), 0.0)
        kernel = kernel * inner_prod[None, :, :] * block_step.T[:, None, :]
        within = jnp.einsum("hij,jhp->ihp", kernel, block_values, precision=HIGHEST)
        carried = (
            jnp.einsum("in,hpn->ihp", block_c, state, precision=HIGHEST)
            * jnp.exp(logdecay)[:, :, None]
        )
        trailing = jnp.exp(logdecay[-1][None, :] - logdecay) * block_step
        update = jnp.einsum("jh,jhp,jn->hpn", trailing, block_values, block_b, precision=HIGHEST)
        new_state = state * jnp.exp(logdecay[-1])[:, None, None] + update
        return (new_state, within + carried)

    start = jnp.zeros((heads, hdim_local, b_map.shape[1]), jnp.float32)
    final_state, outputs = lax.scan(jax.checkpoint(span_step), start, (values_c, step_c, b_c, c_c))
    return outputs.reshape(length, heads, hdim_local)


def mixer(gate_pre, value_pre, shared_pre, step_pre, conv_value, conv_bc, head_params):
    length = gate_pre.shape[0]
    heads = step_pre.shape[1]
    values = jax.nn.silu(causal(value_pre, conv_value))
    shared = jax.nn.silu(causal(shared_pre, conv_bc))
    half_width = shared.shape[1] // 2
    step_size = jax.nn.softplus(step_pre + head_params[0])
    rate = -jnp.exp(head_params[1])
    headed = values.reshape(length, heads, -1)
    scanned = scan_state(headed, step_size, rate, shared[:, :half_width], shared[:, half_width:])
    scanned = scanned + head_params[2][None, :, None] * headed
    return scanned.reshape(length, -1) * jax.nn.silu(gate_pre)


def group_mix(gate_pre, value_pre, shared_pre, step_pre, conv_value, conv_bc, head_params):
    return jax.vmap(mixer, in_axes=(0, 0, 0, 0, None, None, None))(
        gate_pre, value_pre, shared_pre, step_pre, conv_value, conv_bc, head_params
    )


def project(normed, fetched):
    groups = normed.shape[0] // SEQLEN
    outputs = []
    for matrix in fetched[:4]:
        product = jnp.dot(normed, matrix, preferred_element_type=jnp.float32)
        outputs.append(product.reshape(groups, SEQLEN, -1))
    return outputs


def contract_rows(left, right):
    return lax.dot_general(
        left, right, (((0,), (0,)), ((), ())), preferred_element_type=jnp.float32
    )


def contract_cols(left, right):
    return lax.dot_general(
        left, right, (((1,), (1,)), ((), ())), preferred_element_type=jnp.float32
    )


def place(piece, total):
    start = lax.axis_index("tensor") * piece.shape[-1]
    filled = jnp.zeros(piece.shape[:-1] + (total,), jnp.float32)
    return lax.dynamic_update_slice_in_dim(filled, piece, start, piece.ndim - 1)


def pick(whole, width):
    start = lax.axis_index("tensor") * width
    return lax.dynamic_slice_in_dim(whole, start, width, whole.ndim - 1)


def body(
    tokens,
    cotangent,
    norm_gain,
    w_gate,
    w_value,
    w_bc,
    w_step,
    conv_value,
    conv_bc,
    head_params,
    gnorm_gain,
    w_out,
):
    rows32 = tokens.astype(jnp.float32)
    grad_out = cotangent.astype(jnp.float32)
    scaling = lax.rsqrt(jnp.mean(rows32 * rows32, axis=1, keepdims=True) + EPSILON)
    normed = lax.all_gather(
        (rows32 * scaling * norm_gain).astype(jnp.bfloat16), "tensor", axis=0, tiled=True
    )
    fetched = (
        lax.all_gather(w_gate, "dp", axis=0, tiled=True),
        lax.all_gather(w_value, "dp", axis=0, tiled=True),
        lax.all_gather(w_bc, "dp", axis=0, tiled=True),
        lax.all_gather(w_step, "dp", axis=0, tiled=True),
        lax.all_gather(w_out, "dp", axis=1, tiled=True),
    )
    projected = project(normed, fetched)
    mixed_in, mix_back = jax.vjp(
        group_mix,
        projected[0],
        projected[1],
        projected[2],
        projected[3],
        conv_value,
        conv_bc,
        head_params,
    )
    group_rows = normed.shape[0]
    gated = mixed_in.reshape(group_rows, -1)
    total_sq = lax.psum(jnp.sum(gated * gated, axis=1), "tensor")
    rescale = lax.rsqrt(total_sq / INNER + EPSILON)[:, None]
    unitized = gated * rescale
    scaled = (unitized * gnorm_gain).astype(jnp.bfloat16)
    branch = jnp.dot(scaled, fetched[4], preferred_element_type=jnp.float32)
    block_out = rows32 + lax.psum_scatter(
        branch.astype(jnp.bfloat16), "tensor", scatter_dimension=0, tiled=True
    ).astype(jnp.float32)
    grad_rows = lax.all_gather(cotangent, "tensor", axis=0, tiled=True)
    grad_scaled = contract_cols(grad_rows, fetched[4])
    grad_w_out = contract_rows(scaled, grad_rows)
    grad_gnorm_full = place(jnp.sum(grad_scaled * unitized, axis=0), INNER)
    grad_unit = grad_scaled * gnorm_gain
    cross_sum = lax.psum(jnp.sum(grad_unit * gated, axis=1), "tensor")
    grad_gated = (
        rescale * grad_unit - gated * (rescale * rescale * rescale) * cross_sum[:, None] / INNER
    )
    mix_grads = mix_back(grad_gated.reshape(mixed_in.shape))
    grad_normed = jnp.zeros((group_rows, normed.shape[1]), jnp.float32)
    weight_terms = []
    for index in range(4):
        rounded = mix_grads[index].reshape(group_rows, -1).astype(jnp.bfloat16)
        grad_normed = grad_normed + contract_cols(rounded, fetched[index])
        weight_terms.append(contract_rows(normed, rounded))
    grad_h = lax.psum_scatter(
        grad_normed.astype(jnp.bfloat16), "tensor", scatter_dimension=0, tiled=True
    ).astype(jnp.float32)
    scaled_grad = grad_h * norm_gain
    grad_input = (
        grad_out
        + scaling * scaled_grad
        - rows32
        * (scaling * scaling * scaling)
        * jnp.sum(scaled_grad * rows32, axis=1, keepdims=True)
        / D
    )
    grad_norm_local = jnp.sum(grad_h * rows32 * scaling, axis=0)
    summed = (
        lax.psum_scatter(
            weight_terms[0].astype(jnp.bfloat16), "dp", scatter_dimension=0, tiled=True
        ).astype(jnp.float32),
        lax.psum_scatter(
            weight_terms[1].astype(jnp.bfloat16), "dp", scatter_dimension=0, tiled=True
        ).astype(jnp.float32),
        lax.psum_scatter(
            weight_terms[2].astype(jnp.bfloat16), "dp", scatter_dimension=0, tiled=True
        ).astype(jnp.float32),
        lax.psum_scatter(
            weight_terms[3].astype(jnp.bfloat16), "dp", scatter_dimension=0, tiled=True
        ).astype(jnp.float32),
        lax.psum_scatter(
            grad_w_out.astype(jnp.bfloat16), "dp", scatter_dimension=1, tiled=True
        ).astype(jnp.float32),
    )
    grad_w_bc = lax.psum(summed[2].astype(jnp.bfloat16), "tensor").astype(jnp.float32)
    conv_cols = mix_grads[4].shape[1]
    head_cols = mix_grads[6].shape[1]
    small = lax.psum(
        (
            place(mix_grads[4], INNER),
            place(mix_grads[6], HEADS),
            grad_gnorm_full,
            mix_grads[5],
            grad_norm_local,
        ),
        ("dp", "tensor"),
    )
    grad_conv_value = pick(small[0], conv_cols)
    grad_head_params = pick(small[1], head_cols)
    grad_gnorm_gain = pick(small[2], conv_cols)
    return (
        block_out,
        grad_input,
        small[4],
        summed[0],
        summed[1],
        grad_w_bc,
        summed[3],
        grad_conv_value,
        small[3],
        grad_head_params,
        grad_gnorm_gain,
        summed[4],
    )


def solution(mesh):
    in_specs = (
        P(("dp", "tensor"), None),
        P(("dp", "tensor"), None),
        P(),
        P("dp", "tensor"),
        P("dp", "tensor"),
        P("dp", None),
        P("dp", "tensor"),
        P(None, "tensor"),
        P(),
        P(None, "tensor"),
        P("tensor"),
        P("tensor", "dp"),
    )
    out_specs = (
        P(("dp", "tensor"), None),
        P(("dp", "tensor"), None),
        P(),
        P("dp", "tensor"),
        P("dp", "tensor"),
        P("dp", None),
        P("dp", "tensor"),
        P(None, "tensor"),
        P(),
        P(None, "tensor"),
        P("tensor"),
        P("tensor", "dp"),
    )
    return jax.shard_map(body, mesh=mesh, in_specs=in_specs, out_specs=out_specs, check_vma=False)
```

profile of v0, /device:TPU:0, one launch (start us, length us, event | category | flops | bytes accessed | tf_op | source)
XLA Modules:
  0.0 657.5 jit_solution(18267086036678611181)
XLA Ops:
  16.0 10.4 %all_gather.22 = bf16[1024,8]{0,1:T(8,128)(2,1)S(1)} all-gather(bf16[128,8]{0,1:T(8,128)(2,1)S(1)} %copy-done.59), channel_id=1, replica_groups=mesh['dp'=8,'tensor'=4] {'dp'}, dimensions={0}, use_global_device_ids=true | all-gather | bytes 18432 | tf_op jit(solution)/shard_map/all_gather | solution.py:139
  26.4 9.8 %all_gather.24 = bf16[1024,256]{1,0:T(8,128)(2,1)S(1)} all-gather(bf16[128,256]{1,0:T(8,128)(2,1)S(1)} %copy-done.23), channel_id=1, replica_groups=mesh['dp'=8,'tensor'=4] {'dp'}, dimensions={0}, use_global_device_ids=true | all-gather | bytes 589824 | tf_op jit(solution)/shard_map/all_gather | solution.py:138
  36.2 24.3 %all-gather.6.cloned.1.call-done = bf16[1024,1024]{1,0:T(8,128)(2,1)} async-done(((bf16[256,1024]{1,0:T(8,128)(2,1)}), bf16[1024,1024]{1,0:T(8,128)(2,1)}) %all-gather.6.cloned.1.call-update) | async-done | bytes 2097168 | tf_op jit(solution)/shard_map/all_gather | solution.py:132
  65.6 19.1 %all-gather.8.cloned.1.call-done = bf16[1024,512]{1,0:T(8,128)(2,1)} async-done(((bf16[128,512]{1,0:T(8,128)(2,1)}), bf16[1024,512]{1,0:T(8,128)(2,1)}) %all-gather.8.cloned.1.call-update) | async-done | bytes 1048592 | tf_op jit(solution)/shard_map/all_gather | solution.py:137
  87.2 2.7 fusion.137
  89.9 5.1 reshape.1137
  95.0 3.8 copy.149
  98.8 2.9 compare_select_fusion.2
  103.3 44.2 %while.44 = (s32[]{:T(128)}, f32[1,8,64,128]{3,2,1,0:T(8,128)S(1)}, f32[4,1,256,8,64]{2,4,3,1,0:T(8,128)}, f32[4,1,8,64,128]{4,3,2,1,0:T(8,128)}, f32[4,1,256,8]...) while((s32[]{:T(128)}, f32[1,8,64,128]{3,2,1,0:T(8,128)S(1)}, ...), condition=%wide.region_4.5_spmd.clone.clone, body=%wide.region_1.4_spmd.clone.clone.sunk | while | flops 909582336 | bytes 5468616 | solution.py:59
  109.9 4.4 fusion.288
  120.9 4.5 fusion.288
  132.0 4.4 fusion.288
  143.0 4.4 fusion.288
  147.5 3.8 copy.169
  151.3 4.8 reshape.1130
  156.1 6.6 %multiply_reduce_fusion.9 = (f32[1024]{0:T(1024)S(1)}, f32[1024,512]{1,0:T(8,128)}, f32[1024,512]{1,0:T(8,128)}) fusion(f32[1024,512]{1,0:T(8,128)} %reshape.1130, f32[1,1024,512]{2,1,0:T(8,128)S(1)} %get-tuple-element.802, f32[512]{0:T(512)S(1)} %mul.811, bf16[1024,1024]{1,0:T(8,128)(2,1)} %all-gather.6.cloned.1.call-done, ...), kind=kOutput, calls=%fused_computation.199 | convolution fusion | flops 1080556544 | bytes 11540480 | tf_op jit(solution)/shard_map/dot_general | solution.py:87
  162.7 12.0 %psum.56 = f32[1024]{0:T(1024)S(1)} all-reduce(f32[1024]{0:T(1024)S(1)} %get-tuple-element.797), channel_id=1, replica_groups=mesh['dp'=8,'tensor'=4] {'tensor'}, use_global_device_ids=true, to_apply=%region_6.7 | all-reduce | flops 1024 | bytes 8192 | tf_op jit(solution)/shard_map/psum | solution.py:155
  174.7 8.4 %all-gather.14.cloned.1.call-done = bf16[1024,1024]{1,0:T(8,128)(2,1)} async-done(((bf16[256,1024]{1,0:T(8,128)(2,1)}), bf16[1024,1024]{1,0:T(8,128)(2,1)}) %all-gather.14.cloned.1.call-update) | async-done | bytes 2097168 | tf_op jit(solution)/shard_map/all_gather | solution.py:163
  183.1 5.9 multiply_reduce_fusion.3
  189.0 9.4 %psum.57 = f32[1024]{0:T(1024)S(1)} all-reduce(f32[1024]{0:T(1024)S(1)} %get-tuple-element.715), channel_id=1, replica_groups=mesh['dp'=8,'tensor'=4] {'tensor'}, use_global_device_ids=true, to_apply=%region_9.10 | all-reduce | flops 1024 | bytes 8192 | tf_op jit(solution)/shard_map/psum | solution.py:168
  198.4 5.6 fusion.134
  204.0 4.4 reshape.1131
  208.4 3.8 copy.160
  216.1 107.6 %while.43 = (s32[]{:T(128)}, f32[8]{0:T(128)}, f32[1,8,64,128]{3,2,1,0:T(8,128)S(1)}, f32[4,1,256,8,64]{2,4,3,1,0:T(8,128)}, f32[4,1,256,8]{2,3,1,0:T(8,128)}, /...) while((s32[]{:T(128)}, f32[8]{0:T(128)}, ...), condition=%wide.region_23.24_spmd.clone, body=%wide.region_10.23_spmd.clone.sunk | while | flops 2126555136 | bytes 16984652 | solution.py:59
  224.1 4.1 fusion.266
  233.3 2.5 reduce-window.74
  238.7 3.8 fusion.272
  250.5 4.1 fusion.266
  259.7 2.5 reduce-window.74
  265.7 3.8 fusion.272
  277.5 4.1 fusion.266
  292.8 3.8 fusion.272
  304.6 4.1 fusion.266
  319.8 3.8 fusion.272
  331.2 31.3 %reduce-scatter.20.cloned.1.call-done = bf16[128,256]{1,0:T(8,128)(2,1)} async-done(((bf16[1024,256]{1,0:T(8,128)(2,1)}), bf16[128,256]{1,0:T(8,128)(2,1)}) %reduce-scatter.20.cloned.1.call-update) | async-done | bytes 65552 | tf_op jit(solution)/shard_map/reduce_scatter | solution.py:199
  362.6 4.6 convolution_convert_fusion.1
  369.7 2.7 copy.172
  372.4 5.0 reshape.1132
  377.4 4.6 fusion.130
  385.4 3.8 multiply_reduce_fusion.7
  402.6 3.8 convolution_convert_fusion
  409.9 26.4 %all-reduce.30.cloned.1.call-done = bf16[128,256]{1,0:T(8,128)(2,1)} async-done(((bf16[128,256]{1,0:T(8,128)(2,1)}), bf16[128,256]{1,0:T(8,128)(2,1)}) %all-reduce.30.cloned.1.call-update) | async-done | bytes 65552 | tf_op jit(solution)/shard_map/psum | solution.py:209
  437.8 37.8 %reduce-scatter.24.cloned.1.call-done = bf16[128,512]{1,0:T(8,128)(2,1)} async-done(((bf16[1024,512]{1,0:T(8,128)(2,1)}), bf16[128,512]{1,0:T(8,128)(2,1)}) %reduce-scatter.24.cloned.1.call-update) | async-done | bytes 131088
  477.4 38.2 %reduce-scatter.16.cloned.1.call-done = bf16[128,512]{1,0:T(8,128)(2,1)} async-done(((bf16[1024,512]{1,0:T(8,128)(2,1)}), bf16[128,512]{1,0:T(8,128)(2,1)}) %reduce-scatter.16.cloned.1.call-update) | async-done | bytes 131088 | tf_op jit(solution)/shard_map/reduce_scatter | solution.py:193
  517.2 37.9 %reduce-scatter.18.cloned.1.call-done = bf16[128,512]{1,0:T(8,128)(2,1)} async-done(((bf16[1024,512]{1,0:T(8,128)(2,1)}), bf16[128,512]{1,0:T(8,128)(2,1)}) %reduce-scatter.18.cloned.1.call-update) | async-done | bytes 131088 | tf_op jit(solution)/shard_map/reduce_scatter | solution.py:196
  556.8 44.5 %reduce-scatter.14.cloned.1.call-done = bf16[256,1024]{1,0:T(8,128)(2,1)} async-done(((bf16[1024,1024]{1,0:T(8,128)(2,1)}), bf16[256,1024]{1,0:T(8,128)(2,1)}) %reduce-scatter.14.cloned.1.call-update) | async-done | bytes 524304 | tf_op jit(solution)/shard_map/reduce_scatter | solution.py:179
  602.7 43.0 %all-reduce.27 = (f32[1024]{0:T(1024)}, f32[5,2048]{1,0:T(8,128)S(1)}, f32[5,256]{1,0:T(8,128)}, f32[3,32]{1,0:T(4,128)S(1)}, f32[2048]{0:T(1024)S(1)}) all-reduce(f32[1024]{0:T(1024)S(1)} %get-tuple-element.732, f32[5,2048]{1,0:T(8,128)S(1)} %add_dynamic-update-slice_fusion, ...), channel_id=1, replica_groups=mesh['dp'=8,'tensor'=4] {'dp','tensor'}, use_global_device_ids=true, to_apply=%region_27.28 | all-reduce | flops 14688 | bytes 117504 | tf_op jit(solution)/shard_map/psum | solution.py:212
  647.8 3.0 fusion.140
  (444 shorter events, 158.3 us)
Async XLA Ops:
  7.2 7.3 %copy-start.61 = (f32[3,8]{1,0:T(4,128)S(1)}, f32[3,8]{1,0:T(4,128)}, u32[]{:S(2)}) copy-start(f32[3,8]{1,0:T(4,128)} %param.25) | copy-start | bytes 292
  7.2 8.7 %copy-start.58 = (f32[5,256]{1,0:T(8,128)S(1)}, f32[5,256]{1,0:T(8,128)}, u32[]{:S(2)}) copy-start(f32[5,256]{1,0:T(8,128)} %param.24) | copy-start | bytes 15364
  7.2 8.7 %copy-start.56 = (f32[5,512]{1,0:T(8,128)S(1)}, f32[5,512]{1,0:T(8,128)}, u32[]{:S(2)}) copy-start(f32[5,512]{1,0:T(8,128)} %param.23) | copy-start | bytes 30724
  7.2 8.8 %copy-start.59 = (bf16[128,8]{0,1:T(8,128)(2,1)S(1)}, bf16[128,8]{0,1:T(8,128)(2,1)}, u32[]{:S(2)}) copy-start(bf16[128,8]{0,1:T(8,128)(2,1)} %param.22) | copy-start | bytes 6148
  7.2 19.2 %copy-start.23 = (bf16[128,256]{1,0:T(8,128)(2,1)S(1)}, bf16[128,256]{1,0:T(8,128)(2,1)}, u32[]{:S(2)}) copy-start(bf16[128,256]{1,0:T(8,128)(2,1)} %param.21) | copy-start | bytes 196612
  7.2 53.3 %all-gather.6.cloned.1.call-start = ((), (), s32[]{:S(2)}) async-start(), calls=%async_computation.7 | async-start | bytes 2621440 | tf_op jit(solution)/shard_map/all_gather | solution.py:132
  11.7 72.9 %all-gather.8.cloned.1.call-start = ((), (), s32[]{:S(2)}) async-start(), calls=%async_computation.8 | async-start | bytes 1179648 | tf_op jit(solution)/shard_map/all_gather | solution.py:137
  12.5 143.6 %all-gather.10.cloned.1.call-start = ((), (), s32[]{:S(2)}) async-start(), calls=%async_computation.9 | async-start | bytes 1179648 | tf_op jit(solution)/shard_map/all_gather | solution.py:136
  13.2 161.5 %all-gather.12.cloned.1.call-start = ((), (), s32[]{:S(2)}) async-start(), calls=%async_computation.10 | async-start | bytes 1179648 | tf_op jit(solution)/shard_map/all_gather | solution.py:140
  13.8 169.3 %all-gather.14.cloned.1.call-start = ((), (), s32[]{:S(2)}) async-start(), calls=%async_computation.12 | async-start | bytes 2621440 | tf_op jit(solution)/shard_map/all_gather | solution.py:163
  14.4 348.1 %reduce-scatter.20.cloned.1.call-start = ((), (), s32[]{:S(2)}) async-start(), calls=%async_computation.16 | async-start | bytes 589824 | tf_op jit(solution)/shard_map/reduce_scatter | solution.py:199
  15.9 140.2 %copy-start.32 = (f32[512]{0:T(512)}, f32[512]{0:T(512)S(1)}, u32[]{:S(2)}) copy-start(f32[512]{0:T(512)S(1)} %mul.811) | copy-start | bytes 6148
  15.9 47.0 %copy-start.45 = (f32[1,256]{1,0:T(1,128)}, f32[1,256]{1,0:T(1,128)S(1)}, u32[]{:S(2)}) copy-start(f32[1,256]{1,0:T(1,128)S(1)} %get-tuple-element.831) | copy-start | bytes 3076
  15.9 47.0 %copy-start.47 = (f32[1,256]{1,0:T(1,128)}, f32[1,256]{1,0:T(1,128)S(1)}, u32[]{:S(2)}) copy-start(f32[1,256]{1,0:T(1,128)S(1)} %get-tuple-element.832) | copy-start | bytes 3076
  15.9 47.0 %copy-start.49 = (f32[1,256]{1,0:T(1,128)}, f32[1,256]{1,0:T(1,128)S(1)}, u32[]{:S(2)}) copy-start(f32[1,256]{1,0:T(1,128)S(1)} %get-tuple-element.833) | copy-start | bytes 3076
  15.9 47.0 %copy-start.51 = (f32[1,256]{1,0:T(1,128)}, f32[1,256]{1,0:T(1,128)S(1)}, u32[]{:S(2)}) copy-start(f32[1,256]{1,0:T(1,128)S(1)} %get-tuple-element.834) | copy-start | bytes 3076
  16.0 71.2 %copy-start.34 = (f32[1,512]{1,0:T(1,128)}, f32[1,512]{1,0:T(1,128)S(1)}, u32[]{:S(2)}) copy-start(f32[1,512]{1,0:T(1,128)S(1)} %get-tuple-element.826) | copy-start | bytes 6148
  16.0 71.2 %copy-start.36 = (f32[1,512]{1,0:T(1,128)}, f32[1,512]{1,0:T(1,128)S(1)}, u32[]{:S(2)}) copy-start(f32[1,512]{1,0:T(1,128)S(1)} %get-tuple-element.827) | copy-start | bytes 6148
  16.0 71.2 %copy-start.38 = (f32[1,512]{1,0:T(1,128)}, f32[1,512]{1,0:T(1,128)S(1)}, u32[]{:S(2)}) copy-start(f32[1,512]{1,0:T(1,128)S(1)} %get-tuple-element.828) | copy-start | bytes 6148
  16.0 71.2 %copy-start.40 = (f32[1,512]{1,0:T(1,128)}, f32[1,512]{1,0:T(1,128)S(1)}, u32[]{:S(2)}) copy-start(f32[1,512]{1,0:T(1,128)S(1)} %get-tuple-element.829) | copy-start | bytes 6148
  26.4 72.4 %copy-start.19 = (bf16[1024,8]{0,1:T(8,128)(2,1)}, bf16[1024,8]{0,1:T(8,128)(2,1)S(1)}, u32[]{:S(2)}) copy-start(bf16[1024,8]{0,1:T(8,128)(2,1)S(1)} %all_gather.22) | copy-start | bytes 49156
  36.2 26.7 %copy-start.14 = (bf16[1024,256]{1,0:T(8,128)(2,1)}, bf16[1024,256]{1,0:T(8,128)(2,1)S(1)}, u32[]{:S(2)}) copy-start(bf16[1024,256]{1,0:T(8,128)(2,1)S(1)} %all_gather.24) | copy-start | bytes 1572868
  64.5 20.1 %copy-start.6 = (bf16[1024,1024]{1,0:T(8,128)(2,1)S(1)}, bf16[1024,1024]{1,0:T(8,128)(2,1)}, u32[]{:S(2)}) copy-start(bf16[1024,1024]{1,0:T(8,128)(2,1)} %all-gather.6.cloned.1.call-done) | copy-start | bytes 6291460
  89.9 108.5 %copy-start.2 = (f32[1,1024,512]{2,1,0:T(8,128)}, f32[1,1024,512]{2,1,0:T(8,128)S(1)}, u32[]{:S(2)}) copy-start(f32[1,1024,512]{2,1,0:T(8,128)S(1)} %get-tuple-element.802) | copy-start | bytes 6291460
  104.1 5.8 copy-start.24
  115.1 5.8 copy-start.24
  126.2 5.8 copy-start.24
  156.1 27.0 %copy-start.54 = (f32[512]{0:T(512)S(1)}, f32[512]{0:T(512)}, u32[]{:S(2)}) copy-start(f32[512]{0:T(512)} %param.26) | copy-start | bytes 6148
  174.7 23.7 %copy-start.25 = (f32[1024]{0:T(1024)}, f32[1024]{0:T(1024)S(1)}, u32[]{:S(2)}) copy-start(f32[1024]{0:T(1024)S(1)} %get-tuple-element.836) | copy-start | bytes 12292
  174.7 23.7 %copy-start.27 = (f32[1024]{0:T(1024)}, f32[1024]{0:T(1024)S(1)}, u32[]{:S(2)}) copy-start(f32[1024]{0:T(1024)S(1)} %get-tuple-element.835) | copy-start | bytes 12292
  221.2 7.0 %copy-start.18 = (f32[8,256]{1,0:T(8,128)}, f32[8,256]{1,0:T(8,128)S(1)}, u32[]{:S(2)}) copy-start(f32[8,256]{1,0:T(8,128)S(1)} %bitcast_add_fusion.13) | copy-start | bytes 24580 | tf_op jit(solution)/shard_map/transpose(jvp(vmap()))/while
  247.7 7.0 %copy-start.18 = (f32[8,256]{1,0:T(8,128)}, f32[8,256]{1,0:T(8,128)S(1)}, u32[]{:S(2)}) copy-start(f32[8,256]{1,0:T(8,128)S(1)} %bitcast_add_fusion.13) | copy-start | bytes 24580 | tf_op jit(solution)/shard_map/transpose(jvp(vmap()))/while
  274.7 7.0 %copy-start.18 = (f32[8,256]{1,0:T(8,128)}, f32[8,256]{1,0:T(8,128)S(1)}, u32[]{:S(2)}) copy-start(f32[8,256]{1,0:T(8,128)S(1)} %bitcast_add_fusion.13) | copy-start | bytes 24580 | tf_op jit(solution)/shard_map/transpose(jvp(vmap()))/while
  301.7 7.0 %copy-start.18 = (f32[8,256]{1,0:T(8,128)}, f32[8,256]{1,0:T(8,128)S(1)}, u32[]{:S(2)}) copy-start(f32[8,256]{1,0:T(8,128)S(1)} %bitcast_add_fusion.13) | copy-start | bytes 24580 | tf_op jit(solution)/shard_map/transpose(jvp(vmap()))/while
  329.6 32.9 %copy-start.26 = (f32[1024]{0:T(1024)S(1)}, f32[1024]{0:T(1024)}, u32[]{:S(2)}) copy-start(f32[1024]{0:T(1024)} %copy-done.25) | copy-start | bytes 12292
  329.6 32.9 %copy-start.55 = (f32[512]{0:T(512)S(1)}, f32[512]{0:T(512)}, u32[]{:S(2)}) copy-start(f32[512]{0:T(512)} %param.26) | copy-start | bytes 6148
  329.7 78.8 %reduce-scatter.22.cloned.1.call-start = ((), (), s32[]{:S(2)}) async-start(), calls=%async_computation.18 | async-start | bytes 294912
  331.1 105.2 %all-reduce.30.cloned.1.call-start = ((), (), s32[]{:S(2)}) async-start(), calls=%async_computation.17 | async-start | bytes 131072 | tf_op jit(solution)/shard_map/psum | solution.py:209
  362.5 113.1 %reduce-scatter.24.cloned.1.call-start = ((), (), s32[]{:S(2)}) async-start(), calls=%async_computation.19 | async-start | bytes 1179648
  369.6 146.0 %reduce-scatter.16.cloned.1.call-start = ((), (), s32[]{:S(2)}) async-start(), calls=%async_computation.14 | async-start | bytes 1179648 | tf_op jit(solution)/shard_map/reduce_scatter | solution.py:193
  385.3 169.8 %reduce-scatter.18.cloned.1.call-start = ((), (), s32[]{:S(2)}) async-start(), calls=%async_computation.15 | async-start | bytes 1179648 | tf_op jit(solution)/shard_map/reduce_scatter | solution.py:196
  394.4 206.9 %reduce-scatter.14.cloned.1.call-start = ((), (), s32[]{:S(2)}) async-start(), calls=%async_computation.13 | async-start | bytes 2621440 | tf_op jit(solution)/shard_map/reduce_scatter | solution.py:179
  401.0 246.8 %reduce-scatter.12.cloned.1.call-start = ((), (), s32[]{:S(2)}) async-start(), calls=%async_computation.11 | async-start | bytes 2621440 | tf_op jit(solution)/shard_map/reduce_scatter | solution.py:160
  406.4 194.9 %copy-start.5 = (bf16[256,1024]{1,0:T(8,128)(2,1)S(1)}, bf16[256,1024]{1,0:T(8,128)(2,1)}, u32[]{:S(2)}) copy-start(bf16[256,1024]{1,0:T(8,128)(2,1)} %param.16) | copy-start | bytes 1572868
  406.4 194.9 %copy-start.31 = (f32[1024]{0:T(1024)S(1)}, f32[1024]{0:T(1024)}, u32[]{:S(2)}) copy-start(f32[1024]{0:T(1024)} %param.18) | copy-start | bytes 12292
  406.4 194.9 %copy-start.43 = (f32[256]{0:T(256)S(1)}, f32[256]{0:T(256)}, u32[]{:S(2)}) copy-start(f32[256]{0:T(256)} %copy-done.42) | copy-start | bytes 3076
  406.4 241.3 %copy-start.13 = (bf16[256,1024]{1,0:T(8,128)(2,1)S(1)}, bf16[256,1024]{1,0:T(8,128)(2,1)}, u32[]{:S(2)}) copy-start(bf16[256,1024]{1,0:T(8,128)(2,1)} %param.17) | copy-start | bytes 1572868
  406.4 241.3 %copy-start.57 = (f32[256]{0:T(256)S(1)}, f32[256]{0:T(256)}, u32[]{:S(2)}) copy-start(f32[256]{0:T(256)} %get-tuple-element.840) | copy-start | bytes 3076
  (38 other events, 110.5 us)
Sparse Core Ops, SparseCore 0:
  11.9 48.6 all-gather.5
  62.4 22.1 all-gather.7
  86.6 23.4 all-gather.9
  111.8 23.5 all-gather.11
  136.9 46.1 all-gather.13
  329.8 32.6 reduce-scatter.19
  366.4 33.6 reduce-scatter.21
  402.3 33.9 all-reduce.29
  439.8 35.7 reduce-scatter.23
  479.5 35.9 reduce-scatter.15
  519.1 36.0 reduce-scatter.17
  557.4 43.8 reduce-scatter.13
  603.6 44.1 reduce-scatter.11
where the time goes:
time: 665 us; the launch traced here: 657 us
  waiting for transfers between devices  271 us (41%)
  matrix products  129 us (19%)
  blocking collectives  84.6 us (13%)
  other arithmetic  81.1 us (12%)
  local copies, waits for them, and re-layouts  76 us (11%)
  between operations  14.9 us (2%)
    dot_general x12, matrix products, span_step(): within = jnp.einsum('hij,jhp->ihp', kernel, block_values, precision=HIGHEST)  49.3 us
    reduce_scatter x1, waiting for transfers between devices, body(): lax.psum_scatter(grad_normed.astype(jnp.bfloat16), 'tensor', scatter_dime...  44.5 us
    psum x1, blocking collectives, body(): lax.psum((place(mix_grads[4], INNER), place(mix_grads[6], HEADS), grad_gn...  43 us
    unnamed x15, waiting for transfers between devices  40.4 us
    reduce_scatter x1, waiting for transfers between devices, body(): lax.psum_scatter(weight_terms[0].astype(jnp.bfloat16), 'dp', scatter_dime...  38.2 us
    reduce_scatter x1, waiting for transfers between devices, body(): lax.psum_scatter(weight_terms[1].astype(jnp.bfloat16), 'dp', scatter_dime...  37.9 us
    reduce_scatter x1, waiting for transfers between devices, body(): lax.psum_scatter(weight_terms[2].astype(jnp.bfloat16), 'dp', scatter_dime...  31.3 us
    psum x1, waiting for transfers between devices, body(): lax.psum(summed[2].astype(jnp.bfloat16), 'tensor').astype(jnp.float32)  26.4 us
  transfers between devices with their start and end apart: 13, of which 10 were waited for; matrix products, arithmetic and copies ran while one was open for 21% of the time, Pallas kernels for 0%

commit v1 on v0

v1 whole, which is shorter than its diff:
```python
import functools

import jax
import jax.numpy as jnp
from jax import lax
from jax.experimental import pallas as pl
from jax.experimental.pallas import tpu as pltpu
from jax.sharding import PartitionSpec as P

D = 1024
SPAN = 256
SEQLEN = 1024
INNER = 2048
LANES = 128

EPSILON = 1e-05
HIGHEST = lax.Precision.HIGHEST
MESH = pl.DeviceIdType.MESH


def causal(sequence, taps):
    width = taps.shape[0] - 1
    padded = jnp.pad(sequence, ((width - 1, 0), (0, 0)))
    total = jnp.zeros_like(sequence) + taps[width]
    for offset in range(width):
        total = total + taps[offset] * padded[offset : offset + sequence.shape[0]]
    return total


def scan_state(values, step_size, rate, b_map, c_map):
    length, heads, hdim_local = values.shape
    count = length // SPAN
    values_c = values.reshape(count, SPAN, heads, hdim_local)
    step_c = step_size.reshape(count, SPAN, heads)
    b_c = b_map.reshape(count, SPAN, b_map.shape[1])
    c_c = c_map.reshape(count, SPAN, c_map.shape[1])
    lower = (
        lax.broadcasted_iota(jnp.int32, (SPAN, SPAN), 0)
        >= lax.broadcasted_iota(jnp.int32, (SPAN, SPAN), 1)
    )[None, :, :]

    def span_step(state, block):
        block_values, block_step, block_b, block_c = block
        logdecay = jnp.cumsum(block_step * rate[None, :], axis=0)
        heads_first = logdecay.T
        inner_prod = jnp.dot(
            block_c, block_b.T, precision=HIGHEST, preferred_element_type=jnp.float32
        )
        spacing = heads_first[:, :, None] - heads_first[:, None, :]
        kernel = jnp.where(lower, jnp.exp(jnp.where(lower, spacing, -60.0)), 0.0)
        kernel = kernel * inner_prod[None, :, :] * block_step.T[:, None, :]
        within = jnp.einsum("hij,jhp->ihp", kernel, block_values, precision=HIGHEST)
        carried = (
            jnp.einsum("in,hpn->ihp", block_c, state, precision=HIGHEST)
            * jnp.exp(logdecay)[:, :, None]
        )
        trailing = jnp.exp(logdecay[-1][None, :] - logdecay) * block_step
        update = jnp.einsum("jh,jhp,jn->hpn", trailing, block_values, block_b, precision=HIGHEST)
        new_state = state * jnp.exp(logdecay[-1])[:, None, None] + update
        return (new_state, within + carried)

    start = jnp.zeros((heads, hdim_local, b_map.shape[1]), jnp.float32)
    final_state, outputs = lax.scan(jax.checkpoint(span_step), start, (values_c, step_c, b_c, c_c))
    return outputs.reshape(length, heads, hdim_local)


def mixer(gate_pre, value_pre, shared_pre, step_pre, conv_value, conv_bc, head_params):
    length = gate_pre.shape[0]
    heads = step_pre.shape[1]
    values = jax.nn.silu(causal(value_pre, conv_value))
    shared = jax.nn.silu(causal(shared_pre, conv_bc))
    half_width = shared.shape[1] // 2
    step_size = jax.nn.softplus(step_pre + head_params[0])
    rate = -jnp.exp(head_params[1])
    headed = values.reshape(length, heads, -1)
    scanned = scan_state(headed, step_size, rate, shared[:, :half_width], shared[:, half_width:])
    scanned = scanned + head_params[2][None, :, None] * headed
    return scanned.reshape(length, -1) * jax.nn.silu(gate_pre)


def contract_rows(left, right):
    return lax.dot_general(
        left, right, (((0,), (0,)), ((), ())), preferred_element_type=jnp.float32
    )


def contract_cols(left, right):
    return lax.dot_general(
        left, right, (((1,), (1,)), ((), ())), preferred_element_type=jnp.float32
    )


def bits_of(size):
    found, bit = [], 1
    while bit < size:
        found.append(bit)
        bit *= 2
    return found


def flip(index, bit):
    return index + bit - 2 * bit * ((index // bit) % 2)


def flip_all(index, mask, bits):
    for bit in bits:
        if mask & bit:
            index = flip(index, bit)
    return index


def reduce_kernel(
    dp, tensor, bc_at, shared_rows, p_ref, small_ref, out_ref, small_out,
    acc, slots, small_slots, bc_send, bc_slots, tsmall_slots,
    send_sem, recv_sem, ssend, srecv, tsend, trecv,
):
    me, rank = lax.axis_index("dp"), lax.axis_index("tensor")
    bits, tbits = bits_of(dp), bits_of(tensor)
    width = p_ref.shape[2]
    cut = (width // LANES + 1) // 2 * LANES
    halves = ((0, cut), (cut, width - cut))
    orders = (bits, bits[:1] + bits[2:] + bits[1:2])
    count = small_ref.shape[0]
    barrier = pltpu.get_barrier_semaphore()
    for bit in bits:
        pl.semaphore_signal(barrier, inc=1, device_id=(flip(me, bit), rank), device_id_type=MESH)
    for bit in tbits:
        pl.semaphore_signal(barrier, inc=1, device_id=(me, flip(rank, bit)), device_id_type=MESH)
    pl.semaphore_wait(barrier, len(bits) + len(tbits))

    slot_of = {}
    sets = []
    for half in range(2):
        order = orders[half]
        seen, number, phases = 0, 0, []
        for phase, bit in enumerate(order):
            seen |= bit
            kept = [r for r in range(dp) if r & seen == 0]
            if phase + 1 < len(order):
                kept.sort(key=lambda r: -(r & order[phase + 1]))
            phases.append(kept)
            for r in kept:
                slot_of[half, phase, r] = number
                number += 1
        sets.append(phases)

    def copy_of(half, phase, r):
        bit = orders[half][phase]
        at, size = halves[half]
        columns = pl.ds(at, size)
        slot = slot_of[half, phase, r]
        if phase == 0:
            source = p_ref.at[flip_all(me, r | bit, bits), :, columns]
        else:
            source = acc.at[r | bit, :, columns]
        return pltpu.make_async_remote_copy(
            src_ref=source,
            dst_ref=slots.at[slot, :, columns],
            send_sem=send_sem.at[half, slot],
            recv_sem=recv_sem.at[half, slot],
            device_id=(flip(me, bit), rank),
            device_id_type=MESH,
        )

    small_out[...] = small_ref[...]
    copies = []

    def small_copy(phase):
        return pltpu.make_async_remote_copy(
            src_ref=small_out,
            dst_ref=small_slots.at[phase],
            send_sem=ssend.at[phase],
            recv_sem=srecv.at[phase],
            device_id=(flip(me, bits[phase]), rank),
            device_id_type=MESH,
        )

    for r_at in range(len(sets[0][0])):
        for half in range(2):
            copy = copy_of(half, 0, sets[half][0][r_at])
            copy.start()
            copies.append(copy)
    for phase in range(len(bits)):
        small = small_copy(phase)
        small.start()
        small.wait()
        small_out[...] += small_slots[phase]
        for r_at in range(len(sets[0][phase])):
            for half in range(2):
                order = orders[half]
                at, size = halves[half]
                columns = pl.ds(at, size)
                r = sets[half][phase][r_at]
                copy_of(half, phase, r).wait_recv()
                arrived = slots[slot_of[half, phase, r], :, columns].astype(jnp.float32)
                if phase == 0:
                    own = p_ref[flip_all(me, r, bits), :, columns]
                else:
                    own = acc[r, :, columns]
                total = own.astype(jnp.float32) + arrived
                if phase + 1 == len(bits):
                    out_ref[:, columns] = total
                else:
                    acc[r, :, columns] = total.astype(jnp.bfloat16)
                    if r & order[phase + 1]:
                        copy = copy_of(half, phase + 1, r ^ order[phase + 1])
                        copy.start()
                        copies.append(copy)
    bc_cols = pl.ds(bc_at, bc_send.shape[1])
    first = count - shared_rows
    for phase, bit in enumerate(tbits):
        bc_send[...] = out_ref[:, bc_cols].astype(jnp.bfloat16)
        pair = []
        for which, (source, target) in enumerate(
            (
                (bc_send, bc_slots.at[phase]),
                (small_out.at[pl.ds(first, shared_rows)], tsmall_slots.at[phase]),
            )
        ):
            copy = pltpu.make_async_remote_copy(
                src_ref=source,
                dst_ref=target,
                send_sem=tsend.at[phase, which],
                recv_sem=trecv.at[phase, which],
                device_id=(me, flip(rank, bit)),
                device_id_type=MESH,
            )
            copy.start()
            pair.append(copy)
        for copy in pair:
            copy.wait()
        out_ref[:, bc_cols] += bc_slots[phase].astype(jnp.float32)
        small_out[pl.ds(first, shared_rows), :] += tsmall_slots[phase]
    for copy in copies:
        copy.wait_send()


def reduce_all(dp, tensor, packed, small, bc_at, bc_width, shared_rows):
    rows, width = packed.shape
    block = rows // dp
    n, t = len(bits_of(dp)), len(bits_of(tensor))
    vmem = pl.BlockSpec(memory_space=pltpu.VMEM)
    return pl.pallas_call(
        functools.partial(reduce_kernel, dp, tensor, bc_at, shared_rows),
        out_shape=(
            jax.ShapeDtypeStruct((block, width), jnp.float32),
            jax.ShapeDtypeStruct(small.shape, jnp.float32),
        ),
        in_specs=[vmem, vmem],
        out_specs=(vmem, vmem),
        scratch_shapes=[
            pltpu.VMEM((dp, block, width), jnp.bfloat16),
            pltpu.VMEM((dp - 1, block, width), jnp.bfloat16),
            pltpu.VMEM((n,) + small.shape, jnp.float32),
            pltpu.VMEM((block, bc_width), jnp.bfloat16),
            pltpu.VMEM((t, block, bc_width), jnp.bfloat16),
            pltpu.VMEM((t, shared_rows, LANES), jnp.float32),
            pltpu.SemaphoreType.DMA((2, dp - 1)),
            pltpu.SemaphoreType.DMA((2, dp - 1)),
            pltpu.SemaphoreType.DMA((n,)),
            pltpu.SemaphoreType.DMA((n,)),
            pltpu.SemaphoreType.DMA((t, 2)),
            pltpu.SemaphoreType.DMA((t, 2)),
        ],
        compiler_params=pltpu.CompilerParams(
            collective_id=0, has_side_effects=True, vmem_limit_bytes=48 * 1024 * 1024
        ),
    )(packed.reshape(dp, block, width), small)


def as_rows(parts, rows):
    flat = jnp.concatenate([part.reshape(-1) for part in parts])
    return jnp.pad(flat, (0, rows * LANES - flat.shape[0])).reshape(rows, LANES)


def body(
    dp,
    tensor,
    tokens,
    cotangent,
    norm_gain,
    w_gate,
    w_value,
    w_bc,
    w_step,
    conv_value,
    conv_bc,
    head_params,
    gnorm_gain,
    w_out,
):
    width, bc_width, heads = w_gate.shape[1], w_bc.shape[1], w_step.shape[1]
    rows32 = tokens.astype(jnp.float32)
    grad_out = cotangent.astype(jnp.float32)
    scaling = lax.rsqrt(jnp.mean(rows32 * rows32, axis=1, keepdims=True) + EPSILON)
    normed = lax.all_gather(
        (rows32 * scaling * norm_gain).astype(jnp.bfloat16), "tensor", axis=0, tiled=True
    )
    shard = jnp.concatenate(
        [w_gate, w_value, w_bc, jnp.pad(w_step, ((0, 0), (0, LANES - heads))), w_out.T], axis=1
    )
    fetched = lax.all_gather(shard, "dp", axis=0, tiled=True)
    grad_rows = lax.all_gather(cotangent, "tensor", axis=0, tiled=True)
    at = 2 * width + bc_width + LANES
    w_cat, w_out_t = fetched[:, :at], fetched[:, at:]
    projected = jnp.dot(normed, w_cat, preferred_element_type=jnp.float32)
    pieces = (
        projected[:, :width],
        projected[:, width : 2 * width],
        projected[:, 2 * width : 2 * width + bc_width],
        projected[:, 2 * width + bc_width : 2 * width + bc_width + heads],
    )
    gated, mix_back = jax.vjp(mixer, *pieces, conv_value, conv_bc, head_params)
    grad_scaled = jnp.dot(grad_rows, w_out_t, preferred_element_type=jnp.float32)
    grad_unit = grad_scaled * gnorm_gain
    sums = lax.psum(
        jnp.stack([jnp.sum(gated * gated, axis=1), jnp.sum(grad_unit * gated, axis=1)]), "tensor"
    )
    rescale = lax.rsqrt(sums[0] / INNER + EPSILON)[:, None]
    unitized = gated * rescale
    scaled = (unitized * gnorm_gain).astype(jnp.bfloat16)
    branch = contract_cols(scaled, w_out_t)
    block_out = rows32 + lax.psum_scatter(
        branch.astype(jnp.bfloat16), "tensor", scatter_dimension=0, tiled=True
    ).astype(jnp.float32)
    grad_w_out_t = contract_rows(grad_rows, scaled)
    grad_gnorm = jnp.sum(grad_scaled * unitized, axis=0)
    grad_gated = (
        rescale * grad_unit - gated * (rescale * rescale * rescale) * sums[1][:, None] / INNER
    )
    mix_grads = mix_back(grad_gated)
    grad_cat = jnp.concatenate(
        [piece.astype(jnp.bfloat16) for piece in mix_grads[:3]]
        + [jnp.pad(mix_grads[3].astype(jnp.bfloat16), ((0, 0), (0, LANES - heads)))],
        axis=1,
    )
    grad_conv_value, grad_conv_bc, grad_head = mix_grads[4:]
    grad_normed = contract_cols(grad_cat, w_cat)
    grad_h = lax.psum_scatter(
        grad_normed.astype(jnp.bfloat16), "tensor", scatter_dimension=0, tiled=True
    ).astype(jnp.float32)
    scaled_grad = grad_h * norm_gain
    grad_input = (
        grad_out
        + scaling * scaled_grad
        - rows32
        * (scaling * scaling * scaling)
        * jnp.sum(scaled_grad * rows32, axis=1, keepdims=True)
        / D
    )
    grad_norm_local = jnp.sum(grad_h * rows32 * scaling, axis=0)
    weight_terms = jnp.concatenate([contract_rows(normed, grad_cat), grad_w_out_t], axis=1)
    own_parts = [grad_conv_value, grad_gnorm, jnp.pad(grad_head, ((0, 0), (0, LANES - heads)))]
    own_rows = -(-(sum(part.size for part in own_parts)) // (8 * LANES)) * 8
    shared_parts = [grad_conv_bc, grad_norm_local]
    shared_rows = -(-(sum(part.size for part in shared_parts)) // (8 * LANES)) * 8
    small = jnp.concatenate([as_rows(own_parts, own_rows), as_rows(shared_parts, shared_rows)])
    summed, small = reduce_all(
        dp, tensor, weight_terms.astype(jnp.bfloat16), small, 2 * width, bc_width, shared_rows
    )
    own, shared = small[:own_rows].reshape(-1), small[own_rows:].reshape(-1)
    n_conv, n_bc = grad_conv_value.size, grad_conv_bc.size
    return (
        block_out,
        grad_input,
        shared[n_bc : n_bc + norm_gain.shape[0]],
        summed[:, :width],
        summed[:, width : 2 * width],
        summed[:, 2 * width : 2 * width + bc_width],
        summed[:, 2 * width + bc_width : 2 * width + bc_width + heads],
        own[:n_conv].reshape(grad_conv_value.shape),
        shared[:n_bc].reshape(grad_conv_bc.shape),
        own[n_conv + width : n_conv + width + 3 * LANES].reshape(3, LANES)[:, :heads],
        own[n_conv : n_conv + width],
        summed[:, at:].T,
    )


def solution(mesh):
    in_specs = (
        P(("dp", "tensor"), None),
        P(("dp", "tensor"), None),
        P(),
        P("dp", "tensor"),
        P("dp", "tensor"),
        P("dp", None),
        P("dp", "tensor"),
        P(None, "tensor"),
        P(),
        P(None, "tensor"),
        P("tensor"),
        P("tensor", "dp"),
    )
    out_specs = (
        P(("dp", "tensor"), None),
        P(("dp", "tensor"), None),
        P(),
        P("dp", "tensor"),
        P("dp", "tensor"),
        P("dp", None),
        P("dp", "tensor"),
        P(None, "tensor"),
        P(),
        P(None, "tensor"),
        P("tensor"),
        P("tensor", "dp"),
    )
    run = functools.partial(body, mesh.shape["dp"], mesh.shape["tensor"])
    return jax.shard_map(run, mesh=mesh, in_specs=in_specs, out_specs=out_specs, check_vma=False)
```

time: 665 us -> 447 us (0.67)
  waiting for transfers between devices: 271 us -> 105 us
  blocking collectives: 84.6 us -> 11.7 us
  Pallas kernels: 0 us -> 44.3 us
  matrix products: 129 us -> 117 us
  other arithmetic: 81.1 us -> 73.7 us
    reduce_scatter x3 -> x0, waiting for transfers between devices: 107 us -> none  [the longest x1 38.2 us: body(): lax.psum_scatter(weight_terms[0].astype(jnp.bfloat16), 'dp', scatter_dime...]
    psum x3 -> x1, blocking collectives: 64.4 us -> 11.7 us  [body(): lax.psum(jnp.stack([jnp.sum(gated * gated, axis=1), jnp.sum(grad_unit * g...]
    pallas_call x0 -> x1, Pallas kernels: none -> 44.3 us  [reduce_all(): pl.pallas_call(functools.partial(reduce_kernel, dp, tensor, bc_at, shared...]
    unnamed x15 -> x5, waiting for transfers between devices: 40.4 us -> 0.75 us
    psum x1 -> x0, waiting for transfers between devices: 26.4 us -> none  [body(): lax.psum(summed[2].astype(jnp.bfloat16), 'tensor').astype(jnp.float32)]
    reduce_scatter x1, waiting for transfers between devices: 44.5 us -> 21.2 us  [body(): lax.psum_scatter(grad_normed.astype(jnp.bfloat16), 'tensor', scatter_dime...]
    all_gather x1, waiting for transfers between devices: 24.3 us -> 45.6 us  [body(): lax.all_gather((rows32 * scaling * norm_gain).astype(jnp.bfloat16), 'tens...]
    all_gather x2 -> x0, blocking collectives: 20.2 us -> none  [the longest x1 10.4 us: body(): lax.all_gather(w_step, 'dp', axis=0, tiled=True)]
  transfers between devices with their start and end apart: 13 -> 5, of which waited for: 10 -> 3; matrix products, arithmetic and copies ran while one was open for 21% -> 22% of each run, Pallas kernels for 0% -> 10%
where the time goes in v1:
time: 447 us; the launch traced here: 440 us
  matrix products  117 us (26%)
  waiting for transfers between devices  105 us (23%)
  other arithmetic  73.7 us (16%)
  local copies, waits for them, and re-layouts  72.8 us (16%)
  Pallas kernels  44.3 us (10%)
  between operations  14.9 us (3%)
  blocking collectives  11.7 us (3%)
    dot_general x12, matrix products, span_step(): within = jnp.einsum('hij,jhp->ihp', kernel, block_values, precision=HIGHEST)  46 us
    all_gather x1, waiting for transfers between devices, body(): lax.all_gather((rows32 * scaling * norm_gain).astype(jnp.bfloat16), 'tens...  45.6 us
    pallas_call x1, Pallas kernels, reduce_all(): pl.pallas_call(functools.partial(reduce_kernel, dp, tensor, bc_at, shared...  44.3 us
    all_gather x1, waiting for transfers between devices, body(): fetched = lax.all_gather(shard, 'dp', axis=0, tiled=True)  36.9 us
    reduce_scatter x1, waiting for transfers between devices, body(): lax.psum_scatter(grad_normed.astype(jnp.bfloat16), 'tensor', scatter_dime...  21.2 us
    another operation x46, other arithmetic  20.7 us
    unnamed x136, local copies, waits for them, and re-layouts  19 us
    dot_general x16, matrix products, span_step(): jnp.einsum('in,hpn->ihp', block_c, state, precision=HIGHEST)  14.3 us
  transfers between devices with their start and end apart: 5, of which 3 were waited for; matrix products, arithmetic and copies ran while one was open for 22% of the time, Pallas kernels for 10%

profile of v1, /device:TPU:0, one launch (start us, length us, event | category | flops | bytes accessed | tf_op | source)
XLA Modules:
  0.0 440.1 jit_solution(4615027212717280227)
XLA Ops:
  9.3 2.1 fusion.125
  14.5 45.6 %all-gather.4.cloned.1.call-done = bf16[1024,1024]{1,0:T(8,128)(2,1)} async-done(((bf16[256,1024]{1,0:T(8,128)(2,1)}), bf16[1024,1024]{1,0:T(8,128)(2,1)}) %all-gather.4.cloned.1.call-update) | async-done | bytes 2097168 | tf_op jit(solution)/shard_map/all_gather | solution.py:296
  60.1 36.9 %all-gather.6.cloned.1.call-done = bf16[1024,1920]{0,1:T(8,128)(2,1)} async-done(((bf16[128,1920]{0,1:T(8,128)(2,1)}), bf16[1024,1920]{0,1:T(8,128)(2,1)}) %all-gather.6.cloned.1.call-update) | async-done | bytes 3932176 | tf_op jit(solution)/shard_map/all_gather | solution.py:302
  97.0 5.9 %fusion.103 = f32[1024,1408]{1,0:T(8,128)S(1)} fusion(bf16[1024,1024]{1,0:T(8,128)(2,1)} %all-gather.4.cloned.1.call-done, bf16[1024,1920]{0,1:T(8,128)(2,1)} %all-gather.6.cloned.1.call-done), kind=kOutput, calls=%fused_computation.141 | convolution fusion | flops 2952790016 | bytes 10747904 | tf_op jit(solution)/shard_map/dot_general | solution.py:306
  103.1 2.0 slice.263
  108.6 2.7 fusion.113
  111.2 5.2 %reshape.463 = f32[4,256,8,64]{3,2,1,0:T(8,128)} reshape(f32[1024,512]{1,0:T(8,128)} %get-tuple-element.873) | data formatting | bytes 4194304 | tf_op jit(solution)/shard_map/jvp()/reshape;jvp()/reshape | solution.py:33
  116.4 3.9 copy.146
  121.9 36.5 %while.44 = (s32[]{:T(128)}, f32[8,64,128]{2,1,0:T(8,128)S(1)}, f32[4,256,8,64]{1,3,2,0:T(8,128)}, f32[4,8,64,128]{3,2,1,0:T(8,128)}, f32[4,256,8]{1,2,0:T(8,128...) while((s32[]{:T(128)}, f32[8,64,128]{2,1,0:T(8,128)S(1)}, ...), condition=%wide.region_4.5_spmd.clone.clone, body=%wide.region_1.4_spmd.clone.clone.sunk | while | flops 909582336 | bytes 5207435 | solution.py:63
  123.6 3.6 fusion.258
  132.7 3.6 fusion.258
  141.9 3.6 fusion.258
  151.0 3.6 fusion.258
  158.4 3.9 copy.165
  162.3 4.8 %reshape.460 = f32[1024,512]{1,0:T(8,128)} reshape(f32[4,256,8,64]{3,2,1,0:T(8,128)} %copy.165) | data formatting | bytes 4194304 | tf_op jit(solution)/shard_map/jvp()/reshape | solution.py:64
  167.2 7.3 %multiply_reduce_fusion.10 = (f32[1024]{0:T(1024)S(1)}, f32[1024]{0:T(1024)S(1)}, f32[1024,512]{1,0:T(8,128)}, f32[512,1024]{0,1:T(8,128)}) fusion(f32[512]{0:T(512)S(1)} %copy-done.61, f32[1024,1408]{1,0:T(8,128)} %copy-done.4, f32[1024,512]{1,0:T(8,128)} %reshape.460, f32[1024,512]{1,0:T(8,128)S(1)} %get-tuple-element.874, f32[512]{0:T(512)S(1)} %mul.766, ...), kind=kOutput, calls=%fused_computation.169 | convolution fusion | flops 1082128384 | bytes 13643776 | tf_op jit(solution)/shard_map/dot_general | solution.py:314
  174.5 11.7 %psum.7 = f32[2,1024]{1,0:T(2,128)S(1)} all-reduce(f32[2,1024]{1,0:T(2,128)S(1)} %pad_maximum_fusion.2), channel_id=1, replica_groups=mesh['dp'=8,'tensor'=4] {'tensor'}, use_global_device_ids=true, to_apply=%region_7.8 | all-reduce | flops 2048 | bytes 16384 | tf_op jit(solution)/shard_map/psum | solution.py:316
  186.3 6.5 %multiply_reduce_fusion.4 = (f32[512]{0:T(512)}, f32[1024,512]{1,0:T(8,128)}, bf16[1024,512]{1,0:T(8,128)(2,1)}, f32[512]{0:T(512)}) fusion(f32[1024,512]{1,0:T(8,128)S(1)} %get-tuple-element.874, f32[1024,1408]{1,0:T(8,128)} %copy-done.4, f32[1024]{0:T(1024)S(1)} %bitcast.364, f32[1024,512]{1,0:T(8,128)} %get-tuple-element.870, ...), kind=kLoop, calls=%fused_computation.161 | loop fusion | flops 15727616 | bytes 13651968 | tf_op jit(solution)/shard_map/transpose(jvp())/reduce_sum | solution.py:77
  192.8 4.5 %reshape.461 = f32[4,256,8,64]{3,2,1,0:T(8,128)} reshape(f32[1024,512]{1,0:T(8,128)} %get-tuple-element.866) | data formatting | bytes 4194304 | tf_op jit(solution)/shard_map/transpose(jvp())/reshape;transpose(jvp())/reshape | solution.py:64
  197.2 3.8 copy.153
  204.9 98.7 %while.43 = (s32[]{:T(128)}, f32[8]{0:T(128)}, f32[8,64,128]{2,1,0:T(8,128)S(1)}, f32[4,256,8,64]{1,3,2,0:T(8,128)}, f32[4,256,8]{1,2,0:T(8,128)}, /*index=5*/f3...) while((s32[]{:T(128)}, f32[8]{0:T(128)}, ...), condition=%wide.region_22.23_spmd.clone, body=%wide.region_9.22_spmd.clone.sunk | while | flops 2126548992 | bytes 16460644 | solution.py:63
  211.6 4.1 fusion.238
  220.6 2.5 reduce-window.74
  225.4 3.8 fusion.245
  235.6 4.1 fusion.238
  244.6 2.5 reduce-window.74
  250.1 3.8 fusion.245
  260.3 4.1 fusion.238
  269.3 2.5 reduce-window.74
  274.8 3.8 fusion.245
  285.0 4.1 fusion.238
  294.0 2.5 reduce-window.74
  299.5 3.8 fusion.245
  306.4 2.6 multiply_reduce_fusion.14
  309.0 1.7 broadcast_multiply_fusion.4
  311.7 2.8 copy.168
  314.5 5.0 %reshape.462 = f32[1024,512]{1,0:T(8,128)} reshape(f32[4,256,8,64]{3,2,1,0:T(8,128)} %copy.168) | data formatting | bytes 4194304 | tf_op jit(solution)/shard_map/transpose(jvp())/reshape | solution.py:33
  319.5 5.9 %multiply_reduce_fusion.8 = (f32[512]{0:T(512)S(1)}, f32[512]{0:T(512)S(1)}, f32[512]{0:T(512)S(1)}, f32[512]{0:T(512)S(1)}, f32[512]{0:T(512)S(1)}, /*index=5*/f32[1024,512]{1,0:T(8,128)S(1)}) fusion(f32[1024,1408]{1,0:T(8,128)} %copy-done.4, f32[1024,512]{1,0:T(8,128)} %slice.263, f32[1024,512]{1,0:T(8,128)S(1)} %copy-done.2, f32[1024,512]{1,0:T(8,128)} %reshape.462, ...), kind=kLoop, calls=%fused_computation.165 | loop fusion | flops 10483200 | bytes 12595200 | tf_op jit(solution)/shard_map/transpose(jvp())/reduce_sum | solution.py:26
  330.7 4.6 %fusion.114 = bf16[1024,1024]{1,0:T(8,128)(2,1)} fusion(bf16[1024,1920]{0,1:T(8,128)(2,1)S(1)} %copy-done.65, bf16[1024,8]{1,0:T(8,128)(2,1)S(1)} %get-tuple-element.868, bf16[1024,256]{1,0:T(8,128)(2,1)S(1)} %fusion.131, bf16[1024,512]{1,0:T(8,128)(2,1)S(1)} %fusion.110, bf16[1024,512]{1,0:T(8,128)(2,1)S(1)} %copy-done.18), kind=kOutput, calls=%fused_computation.178 | convolution fusion | flops 2968256512 | bytes 7864320 | tf_op jit(solution)/shard_map/dot_general | solution.py:88
  336.8 3.9 convolution_convert_fusion.1
  340.7 3.9 fusion.117
  344.7 1.8 copy.157
  347.5 5.4 %convolution_convert_fusion = bf16[1024,1408]{1,0:T(8,128)(2,1)S(1)} fusion(bf16[1024,1024]{1,0:T(8,128)(2,1)} %all-gather.4.cloned.1.call-done, bf16[1024,8]{1,0:T(8,128)(2,1)S(1)} %get-tuple-element.868, bf16[1024,256]{1,0:T(8,128)(2,1)S(1)} %copy-done.23, bf16[1024,512]{1,0:T(8,128)(2,1)} %copy-done.20, bf16[1024,512]{1,0:T(8,128)(2,1)S(1)} %copy-done.19), kind=kOutput, calls=%fused_computation.135 | convolution fusion | flops 2968649728 | bytes 7618560 | tf_op jit(solution)/shard_map/dot_general | solution.py:82
  353.0 2.4 pad_maximum_fusion.p_ref
  355.3 21.2 %reduce-scatter.5.cloned.1.call-done = bf16[256,1024]{1,0:T(8,128)(2,1)} async-done(((bf16[1024,1024]{1,0:T(8,128)(2,1)}), bf16[256,1024]{1,0:T(8,128)(2,1)}) %reduce-scatter.5.cloned.1.call-update) | async-done | bytes 524304 | tf_op jit(solution)/shard_map/reduce_scatter | solution.py:339
  378.0 2.1 copy-done
  380.1 44.3 %shard_map.211 = (f32[128,1920]{1,0:T(8,128)S(1)}, f32[56,128]{1,0:T(8,128)S(1)}) custom-call(bf16[8,128,1920]{2,1,0:T(8,128)(2,1)S(1)} %copy-done, f32[56,128]{1,0:T(8,128)S(1)} %pad_maximum_fusion.1.small_ref), custom_call_target="tpu_custom_call" | custom-call | tf_op jit(solution)/shard_map/pallas_call | solution.py:243
  430.5 2.8 fusion.120
  (427 shorter events, 111.0 us)
Async XLA Ops:
  7.2 4.2 copy-start.28
  7.2 4.3 copy-start.25
  7.2 4.5 %copy-start.26 = (bf16[128,512]{1,0:T(8,128)(2,1)S(1)}, bf16[128,512]{1,0:T(8,128)(2,1)}, u32[]{:S(2)}) copy-start(bf16[128,512]{1,0:T(8,128)(2,1)} %param.20) | copy-start | bytes 393220
  7.2 4.7 %copy-start.63 = (bf16[128,8]{0,1:T(8,128)(2,1)S(1)}, bf16[128,8]{0,1:T(8,128)(2,1)}, u32[]{:S(2)}) copy-start(bf16[128,8]{0,1:T(8,128)(2,1)} %param.22) | copy-start | bytes 6148
  7.2 4.7 %copy-start.27 = (bf16[512,128]{1,0:T(8,128)(2,1)S(1)}, bf16[512,128]{1,0:T(8,128)(2,1)}, u32[]{:S(2)}) copy-start(bf16[512,128]{1,0:T(8,128)(2,1)} %param.27) | copy-start | bytes 393220
  7.2 52.9 %all-gather.4.cloned.1.call-start = ((), (), s32[]{:S(2)}) async-start(), calls=%async_computation.2 | async-start | bytes 2621440 | tf_op jit(solution)/shard_map/all_gather | solution.py:296
  9.2 4.3 copy-start.64
  9.2 5.1 %copy-start.60 = (f32[5,256]{1,0:T(8,128)S(1)}, f32[5,256]{1,0:T(8,128)}, u32[]{:S(2)}) copy-start(f32[5,256]{1,0:T(8,128)} %param.24) | copy-start | bytes 15364
  9.3 5.1 %copy-start.57 = (f32[5,512]{1,0:T(8,128)S(1)}, f32[5,512]{1,0:T(8,128)}, u32[]{:S(2)}) copy-start(f32[5,512]{1,0:T(8,128)} %param.23) | copy-start | bytes 30724
  11.3 85.7 %all-gather.6.cloned.1.call-start = ((), (), s32[]{:S(2)}) async-start(), calls=%async_computation.3 | async-start | bytes 4423680 | tf_op jit(solution)/shard_map/all_gather | solution.py:302
  12.7 154.4 %all-gather.8.cloned.1.call-start = ((), (), s32[]{:S(2)}) async-start(), calls=%async_computation.4 | async-start | bytes 2621440 | tf_op jit(solution)/shard_map/all_gather | solution.py:303
  13.5 363.1 %reduce-scatter.5.cloned.1.call-start = ((), (), s32[]{:S(2)}) async-start(), calls=%async_computation.6 | async-start | bytes 2621440 | tf_op jit(solution)/shard_map/reduce_scatter | solution.py:339
  13.6 91.5 %copy-start.58 = (f32[8]{0:T(128)}, f32[8]{0:T(128)S(1)}, u32[]{:S(2)}) copy-start(f32[8]{0:T(128)S(1)} %get-tuple-element.914) | copy-start | bytes 100
  14.4 171.9 %copy-start.42 = (f32[512]{0:T(512)}, f32[512]{0:T(512)S(1)}, u32[]{:S(2)}) copy-start(f32[512]{0:T(512)S(1)} %mul.766) | copy-start | bytes 6148
  14.4 92.2 %copy-start.47 = (f32[1,256]{1,0:T(1,128)}, f32[1,256]{1,0:T(1,128)S(1)}, u32[]{:S(2)}) copy-start(f32[1,256]{1,0:T(1,128)S(1)} %get-tuple-element.909) | copy-start | bytes 3076
  14.4 92.2 %copy-start.49 = (f32[1,256]{1,0:T(1,128)}, f32[1,256]{1,0:T(1,128)S(1)}, u32[]{:S(2)}) copy-start(f32[1,256]{1,0:T(1,128)S(1)} %get-tuple-element.910) | copy-start | bytes 3076
  14.4 92.2 %copy-start.51 = (f32[1,256]{1,0:T(1,128)}, f32[1,256]{1,0:T(1,128)S(1)}, u32[]{:S(2)}) copy-start(f32[1,256]{1,0:T(1,128)S(1)} %get-tuple-element.911) | copy-start | bytes 3076
  14.4 92.2 %copy-start.53 = (f32[1,256]{1,0:T(1,128)}, f32[1,256]{1,0:T(1,128)S(1)}, u32[]{:S(2)}) copy-start(f32[1,256]{1,0:T(1,128)S(1)} %get-tuple-element.912) | copy-start | bytes 3076
  14.5 93.9 %copy-start.34 = (f32[1,512]{1,0:T(1,128)}, f32[1,512]{1,0:T(1,128)S(1)}, u32[]{:S(2)}) copy-start(f32[1,512]{1,0:T(1,128)S(1)} %get-tuple-element.902) | copy-start | bytes 6148
  14.5 93.9 %copy-start.36 = (f32[1,512]{1,0:T(1,128)}, f32[1,512]{1,0:T(1,128)S(1)}, u32[]{:S(2)}) copy-start(f32[1,512]{1,0:T(1,128)S(1)} %get-tuple-element.903) | copy-start | bytes 6148
  14.5 93.9 %copy-start.38 = (f32[1,512]{1,0:T(1,128)}, f32[1,512]{1,0:T(1,128)S(1)}, u32[]{:S(2)}) copy-start(f32[1,512]{1,0:T(1,128)S(1)} %get-tuple-element.904) | copy-start | bytes 6148
  14.5 93.9 %copy-start.40 = (f32[1,512]{1,0:T(1,128)}, f32[1,512]{1,0:T(1,128)S(1)}, u32[]{:S(2)}) copy-start(f32[1,512]{1,0:T(1,128)S(1)} %get-tuple-element.905) | copy-start | bytes 6148
  111.2 75.0 %copy-start.1 = (f32[1024,512]{1,0:T(8,128)}, f32[1024,512]{1,0:T(8,128)S(1)}, u32[]{:S(2)}) copy-start(f32[1024,512]{1,0:T(8,128)S(1)} %get-tuple-element.874) | copy-start | bytes 6291460
  162.3 4.8 %copy-start.61 = (f32[512]{0:T(512)S(1)}, f32[512]{0:T(512)}, u32[]{:S(2)}) copy-start(f32[512]{0:T(512)} %param.26) | copy-start | bytes 6148
  186.2 6.5 %copy-start.31 = (f32[1,1024]{1,0:T(1,128)}, f32[1,1024]{1,0:T(1,128)S(1)}, u32[]{:S(2)}) copy-start(f32[1,1024]{1,0:T(1,128)S(1)} %get-tuple-element.907) | copy-start | bytes 12292
  201.0 3.9 copy-start.9
  208.7 7.0 %copy-start.24 = (f32[8,256]{1,0:T(8,128)}, f32[8,256]{1,0:T(8,128)S(1)}, u32[]{:S(2)}) copy-start(f32[8,256]{1,0:T(8,128)S(1)} %add_bitcast_fusion.8) | copy-start | bytes 24580 | tf_op jit(solution)/shard_map/transpose(jvp())/while
  211.5 4.1 copy-start.10
  232.7 7.0 %copy-start.24 = (f32[8,256]{1,0:T(8,128)}, f32[8,256]{1,0:T(8,128)S(1)}, u32[]{:S(2)}) copy-start(f32[8,256]{1,0:T(8,128)S(1)} %add_bitcast_fusion.8) | copy-start | bytes 24580 | tf_op jit(solution)/shard_map/transpose(jvp())/while
  235.6 4.1 copy-start.10
  257.4 7.0 %copy-start.24 = (f32[8,256]{1,0:T(8,128)}, f32[8,256]{1,0:T(8,128)S(1)}, u32[]{:S(2)}) copy-start(f32[8,256]{1,0:T(8,128)S(1)} %add_bitcast_fusion.8) | copy-start | bytes 24580 | tf_op jit(solution)/shard_map/transpose(jvp())/while
  260.3 4.1 copy-start.10
  282.1 7.0 %copy-start.24 = (f32[8,256]{1,0:T(8,128)}, f32[8,256]{1,0:T(8,128)S(1)}, u32[]{:S(2)}) copy-start(f32[8,256]{1,0:T(8,128)S(1)} %add_bitcast_fusion.8) | copy-start | bytes 24580 | tf_op jit(solution)/shard_map/transpose(jvp())/while
  285.0 4.1 copy-start.10
  314.5 5.0 %copy-start.2 = (f32[1024,512]{1,0:T(8,128)S(1)}, f32[1024,512]{1,0:T(8,128)}, u32[]{:S(2)}) copy-start(f32[1024,512]{1,0:T(8,128)} %copy-done.1) | copy-start | bytes 6291460
  314.5 5.0 %copy-start.43 = (f32[512]{0:T(512)S(1)}, f32[512]{0:T(512)}, u32[]{:S(2)}) copy-start(f32[512]{0:T(512)} %copy-done.42) | copy-start | bytes 6148
  319.5 5.9 %copy-start.35 = (f32[1,512]{1,0:T(1,128)S(1)}, f32[1,512]{1,0:T(1,128)}, u32[]{:S(2)}) copy-start(f32[1,512]{1,0:T(1,128)} %copy-done.34) | copy-start | bytes 6148
  319.5 5.9 %copy-start.37 = (f32[1,512]{1,0:T(1,128)S(1)}, f32[1,512]{1,0:T(1,128)}, u32[]{:S(2)}) copy-start(f32[1,512]{1,0:T(1,128)} %copy-done.36) | copy-start | bytes 6148
  319.5 5.9 %copy-start.39 = (f32[1,512]{1,0:T(1,128)S(1)}, f32[1,512]{1,0:T(1,128)}, u32[]{:S(2)}) copy-start(f32[1,512]{1,0:T(1,128)} %copy-done.38) | copy-start | bytes 6148
  319.5 5.9 %copy-start.41 = (f32[1,512]{1,0:T(1,128)S(1)}, f32[1,512]{1,0:T(1,128)}, u32[]{:S(2)}) copy-start(f32[1,512]{1,0:T(1,128)} %copy-done.40) | copy-start | bytes 6148
  330.7 4.6 %copy-start.32 = (f32[1,1024]{1,0:T(1,128)S(1)}, f32[1,1024]{1,0:T(1,128)}, u32[]{:S(2)}) copy-start(f32[1,1024]{1,0:T(1,128)} %copy-done.31) | copy-start | bytes 12292
  335.3 95.2 %reduce-scatter.3.cloned.1.call-start = ((), (), s32[]{:S(2)}) async-start(), calls=%async_computation.5 | async-start | bytes 2621440 | tf_op jit(solution)/shard_map/reduce_scatter | solution.py:323
  352.9 23.7 %copy-start.8 = (bf16[256,1024]{1,0:T(8,128)(2,1)S(1)}, bf16[256,1024]{1,0:T(8,128)(2,1)}, u32[]{:S(2)}) copy-start(bf16[256,1024]{1,0:T(8,128)(2,1)} %param.16) | copy-start | bytes 1572868
  352.9 23.7 %copy-start.33 = (f32[1024]{0:T(1024)S(1)}, f32[1024]{0:T(1024)}, u32[]{:S(2)}) copy-start(f32[1024]{0:T(1024)} %param.18) | copy-start | bytes 12292
  353.0 23.6 %copy-start.45 = (f32[256]{0:T(256)S(1)}, f32[256]{0:T(256)}, u32[]{:S(2)}) copy-start(f32[256]{0:T(256)} %copy-done.44) | copy-start | bytes 3076
  424.5 6.0 %copy-start.15 = (bf16[256,1024]{1,0:T(8,128)(2,1)S(1)}, bf16[256,1024]{1,0:T(8,128)(2,1)}, u32[]{:S(2)}) copy-start(bf16[256,1024]{1,0:T(8,128)(2,1)} %param.17) | copy-start | bytes 1572868
  424.5 6.0 %copy-start.16 = (bf16[256,1024]{1,0:T(8,128)(2,1)S(1)}, bf16[256,1024]{1,0:T(8,128)(2,1)}, u32[]{:S(2)}) copy-start(bf16[256,1024]{1,0:T(8,128)(2,1)} %reduce-scatter.5.cloned.1.call-done) | copy-start | bytes 1572868
  424.5 6.0 %copy-start.59 = (f32[256]{0:T(256)S(1)}, f32[256]{0:T(256)}, u32[]{:S(2)}) copy-start(f32[256]{0:T(256)} %get-tuple-element.916) | copy-start | bytes 3076
  (35 other events, 85.5 us)
Sparse Core Ops, SparseCore 0:
  11.5 48.6 all-gather.3
  62.0 34.9 all-gather.5
  98.6 45.9 all-gather.7
  335.4 41.1 reduce-scatter.4
  378.8 46.4 reduce-scatter.2

commit v2 on v1

--- a/solution.py
+++ b/solution.py
@@ -30,38 +30,36 @@
 def scan_state(values, step_size, rate, b_map, c_map):
     length, heads, hdim_local = values.shape
     count = length // SPAN
-    values_c = values.reshape(count, SPAN, heads, hdim_local)
-    step_c = step_size.reshape(count, SPAN, heads)
+    dots = functools.partial(
+        jnp.einsum, precision=lax.Precision.HIGH, preferred_element_type=jnp.float32
+    )
+    step_c = step_size.reshape(count, SPAN, heads).transpose(0, 2, 1)
+    scaled_c = values.reshape(count, SPAN, heads, hdim_local).transpose(0, 2, 1, 3)
+    scaled_c = scaled_c * step_c[:, :, :, None]
     b_c = b_map.reshape(count, SPAN, b_map.shape[1])
     c_c = c_map.reshape(count, SPAN, c_map.shape[1])
     lower = (
         lax.broadcasted_iota(jnp.int32, (SPAN, SPAN), 0)
         >= lax.broadcasted_iota(jnp.int32, (SPAN, SPAN), 1)
-    )[None, :, :]
-
-    def span_step(state, block):
-        block_values, block_step, block_b, block_c = block
-        logdecay = jnp.cumsum(block_step * rate[None, :], axis=0)
-        heads_first = logdecay.T
-        inner_prod = jnp.dot(
-            block_c, block_b.T, precision=HIGHEST, preferred_element_type=jnp.float32
-        )
-        spacing = heads_first[:, :, None] - heads_first[:, None, :]
-        kernel = jnp.where(lower, jnp.exp(jnp.where(lower, spacing, -60.0)), 0.0)
-        kernel = kernel * inner_prod[None, :, :] * block_step.T[:, None, :]
-        within = jnp.einsum("hij,jhp->ihp", kernel, block_values, precision=HIGHEST)
-        carried = (
-            jnp.einsum("in,hpn->ihp", block_c, state, precision=HIGHEST)
-            * jnp.exp(logdecay)[:, :, None]
-        )
-        trailing = jnp.exp(logdecay[-1][None, :] - logdecay) * block_step
-        update = jnp.einsum("jh,jhp,jn->hpn", trailing, block_values, block_b, precision=HIGHEST)
-        new_state = state * jnp.exp(logdecay[-1])[:, None, None] + update
-        return (new_state, within + carried)
-
-    start = jnp.zeros((heads, hdim_local, b_map.shape[1]), jnp.float32)
-    final_state, outputs = lax.scan(jax.checkpoint(span_step), start, (values_c, step_c, b_c, c_c))
-    return outputs.reshape(length, heads, hdim_local)
+    )
+    logdecay = jnp.einsum(
+        "chj,ij->chi", step_c * rate[None, :, None], lower.astype(jnp.float32), precision=HIGHEST
+    )
+    inner_prod = dots("cin,cjn->cij", c_c, b_c)
+    spacing = logdecay[:, :, :, None] - logdecay[:, :, None, :]
+    kernel = jnp.where(lower, jnp.exp(jnp.where(lower, spacing, -60.0)), 0.0)
+    within = dots("chij,chjp->chip", kernel * inner_prod[:, None], scaled_c)
+    last = logdecay[:, :, -1]
+    trailing = jnp.exp(last[:, :, None] - logdecay)
+    update = dots("chjp,cjn->chpn", scaled_c * trailing[:, :, :, None], b_c)
+    fade = jnp.exp(last)
+    state = jnp.zeros_like(update[0])
+    states = []
+    for index in range(count):
+        states.append(state)
+        state = state * fade[index][:, None, None] + update[index]
+    carried = dots("cin,chpn->chip", c_c, jnp.stack(states)) * jnp.exp(logdecay)[:, :, :, None]
+    return (within + carried).transpose(0, 2, 1, 3).reshape(length, heads, hdim_local)
 
 
 def mixer(gate_pre, value_pre, shared_pre, step_pre, conv_value, conv_bc, head_params):

time: 447 us -> 348 us (0.78)
  matrix products: 117 us -> 65.7 us
  other arithmetic: 73.7 us -> 45.8 us
  local copies, waits for them, and re-layouts: 72.8 us -> 53.9 us
    dot_general x56 -> x14, matrix products: 85.6 us -> 34.9 us  [the longest x3 21 us: scan_state(): within = dots('chij,chjp->chip', kernel * inner_prod[:, None], scaled_c)]
    another operation x50 -> x2, other arithmetic: 20.8 us -> 1.48 us
    squeeze x16 -> x0, local copies, waits for them, and re-layouts: 9.22 us -> none  [scan_state(): lax.scan(jax.checkpoint(span_step), start, (values_c, step_c, b_c, c_c))]
    dynamic_update_slice x8 -> x0, other arithmetic: 8.44 us -> none  [scan_state(): lax.scan(jax.checkpoint(span_step), start, (values_c, step_c, b_c, c_c))]
    unnamed x136 -> x167, local copies, waits for them, and re-layouts: 19 us -> 12.4 us
    another operation x28 -> x1, local copies, waits for them, and re-layouts: 6.58 us -> 0.01 us  [scan_state(): jnp.stack(states)]
    reshape x10 -> x9, local copies, waits for them, and re-layouts: 26.5 us -> 32.4 us  [the longest x4 16.3 us: scan_state(): values.reshape(count, SPAN, heads, hdim_local).transpose(0, 2, 1, 3)]
  transfers between devices with their start and end apart: 5 -> 5, of which waited for: 3 -> 4; matrix products, arithmetic and copies ran while one was open for 22% -> 21% of each run, Pallas kernels for 10% -> 13%
where the time goes in v2:
time: 348 us; the launch traced here: 343 us
  waiting for transfers between devices  106 us (30%)
  matrix products  65.7 us (19%)
  local copies, waits for them, and re-layouts  53.9 us (15%)
  other arithmetic  45.8 us (13%)
  Pallas kernels  44.3 us (13%)
  between operations  15.2 us (4%)
  blocking collectives  10.8 us (3%)
    all_gather x1, waiting for transfers between devices, body(): lax.all_gather((rows32 * scaling * norm_gain).astype(jnp.bfloat16), 'tens...  45.6 us
    pallas_call x1, Pallas kernels, reduce_all(): pl.pallas_call(functools.partial(reduce_kernel, dp, tensor, bc_at, shared...  44.3 us
    all_gather x1, waiting for transfers between devices, body(): fetched = lax.all_gather(shard, 'dp', axis=0, tiled=True)  37.5 us
    reduce_scatter x1, waiting for transfers between devices, body(): lax.psum_scatter(grad_normed.astype(jnp.bfloat16), 'tensor', scatter_dime...  21.4 us
    dot_general x3, matrix products, scan_state(): within = dots('chij,chjp->chip', kernel * inner_prod[:, None], scaled_c)  21 us
    reshape x4, local copies, waits for them, and re-layouts, scan_state(): values.reshape(count, SPAN, heads, hdim_local).transpose(0, 2, 1, 3)  16.3 us
    reshape x4, local copies, waits for them, and re-layouts, scan_state(): (within + carried).transpose(0, 2, 1, 3).reshape(length, heads, hdim_local)  15.9 us
    unnamed x167, local copies, waits for them, and re-layouts  12.4 us
  transfers between devices with their start and end apart: 5, of which 4 were waited for; matrix products, arithmetic and copies ran while one was open for 21% of the time, Pallas kernels for 13%

profile of v2, /device:TPU:0, one launch (start us, length us, event | category | flops | bytes accessed | tf_op | source)
XLA Modules:
  0.0 342.5 jit_solution(13712578192971801424)
XLA Ops:
  7.3 1.4 fusion.66
  9.3 2.1 fusion.68
  14.5 45.6 %all-gather.4.cloned.1.call-done = bf16[1024,1024]{1,0:T(8,128)(2,1)} async-done(((bf16[256,1024]{1,0:T(8,128)(2,1)}), bf16[1024,1024]{1,0:T(8,128)(2,1)}) %all-gather.4.cloned.1.call-update) | async-done | bytes 2097168 | tf_op jit(solution)/shard_map/all_gather | solution.py:294
  60.1 37.5 %all-gather.6.cloned.1.call-done = bf16[1024,1920]{0,1:T(8,128)(2,1)} async-done(((bf16[128,1920]{0,1:T(8,128)(2,1)}), bf16[1024,1920]{0,1:T(8,128)(2,1)}) %all-gather.6.cloned.1.call-update) | async-done | bytes 3932176 | tf_op jit(solution)/shard_map/all_gather | solution.py:300
  97.6 5.9 %fusion.24 = f32[1024,1408]{1,0:T(8,128)S(1)} fusion(bf16[1024,1024]{1,0:T(8,128)(2,1)} %all-gather.4.cloned.1.call-done, bf16[1024,1920]{0,1:T(8,128)(2,1)} %all-gather.6.cloned.1.call-done), kind=kOutput, calls=%fused_computation.30 | convolution fusion | flops 2952790016 | bytes 10747904 | tf_op jit(solution)/shard_map/dot_general | solution.py:304
  103.6 1.9 slice.215
  105.5 1.2 copy-done.5
  107.2 6.2 %fusion.44 = (f32[1024,512]{1,0:T(8,128)}, f32[1024,512]{1,0:T(8,128)S(1)}) fusion(f32[1024,512]{1,0:T(8,128)} %slice.215, f32[512]{0:T(512)S(1)} %bitcast.256, f32[512]{0:T(512)S(1)} %bitcast.258, f32[512]{0:T(512)S(1)} %bitcast.252, f32[512]{0:T(512)S(1)} %bitcast.254, f32[512]{0:T(512)S(1)} %bitcast.269), kind=kLoop, calls=%fused_computation.81 | loop fusion | flops 6291456 | bytes 6301696 | tf_op jit(solution)/shard_map/jvp(jit(silu))/mul | solution.py:68
  113.8 4.7 %reshape.293 = f32[4,256,8,64]{3,2,1,0:T(8,128)} reshape(f32[1024,512]{1,0:T(8,128)} %get-tuple-element.116) | data formatting | bytes 4194304 | tf_op jit(solution)/shard_map/jvp()/reshape;jvp()/reshape | solution.py:37
  118.6 3.8 %copy.115 = f32[4,256,8,64]{1,3,2,0:T(8,128)} copy(f32[4,256,8,64]{3,2,1,0:T(8,128)} %reshape.293) | data formatting | bytes 4194304 | tf_op jit(solution)/shard_map/jvp()/reshape;jvp()/reshape | solution.py:37
  122.6 1.6 fusion.84
  127.2 1.3 copy-done.10
  128.5 6.8 %fusion.42 = f32[4,256,8,64]{1,3,2,0:T(8,128)} fusion(f32[4,8,64,256]{3,2,1,0:T(8,128)S(1)} %fusion.89, f32[4,256,256]{2,1,0:T(8,128)S(1)} %fusion.146, f32[4,8,256]{2,1,0:T(8,128)S(1)} %fusion.101, pred[256,256]{1,0:T(8,128)(4,1)S(1)} %copy-done.33, f32[4,256,8,64]{1,3,2,0:T(8,128)S(1)} %copy-done.3, f32[4,256,8]{1,2,0:T(8,128)S(1)} %get-tuple-element.141, ...), kind=kOutput, calls=%fused_computation.66 | convolution fusion | flops 815267840 | bytes 7503872 | tf_op jit(solution)/shard_map/jvp(chij,chjp->chip)/dot_general | solution.py:51
  135.3 3.9 %copy.139 = f32[4,256,8,64]{3,2,1,0:T(8,128)} copy(f32[4,256,8,64]{1,3,2,0:T(8,128)} %fusion.42) | data formatting | bytes 4194304 | tf_op jit(solution)/shard_map/jvp()/reshape | solution.py:62
  139.2 4.8 %reshape.294 = f32[1024,512]{1,0:T(8,128)} reshape(f32[4,256,8,64]{3,2,1,0:T(8,128)} %copy.139) | data formatting | bytes 4194304 | tf_op jit(solution)/shard_map/jvp()/reshape | solution.py:62
  144.0 1.2 all-gather.8.cloned.1.call-done
  145.2 7.2 %multiply_reduce_fusion.7 = (f32[1024]{0:T(1024)S(1)}, f32[1024]{0:T(1024)S(1)}, f32[1024,512]{1,0:T(8,128)}, f32[512,1024]{0,1:T(8,128)}) fusion(f32[512]{0:T(512)S(1)} %copy-done.69, f32[1024,1408]{1,0:T(8,128)} %copy-done.5, f32[1024,512]{1,0:T(8,128)} %reshape.294, f32[1024,512]{1,0:T(8,128)S(1)} %get-tuple-element.117, f32[512]{0:T(512)S(1)} %mul.618, ...), kind=kOutput, calls=%fused_computation.76 | convolution fusion | flops 1082128384 | bytes 13643776 | tf_op jit(solution)/shard_map/dot_general | solution.py:312
  153.0 10.8 %psum.7 = f32[2,1024]{1,0:T(2,128)S(1)} all-reduce(f32[2,1024]{1,0:T(2,128)} %pad_maximum_fusion.5), channel_id=1, replica_groups=mesh['dp'=8,'tensor'=4] {'tensor'}, use_global_device_ids=true, to_apply=%region_3.4 | all-reduce | flops 2048 | bytes 16384 | tf_op jit(solution)/shard_map/psum | solution.py:314
  163.9 6.0 %multiply_reduce_fusion.1 = (f32[512]{0:T(512)S(1)}, f32[1024,512]{1,0:T(8,128)}, bf16[1024,512]{1,0:T(8,128)(2,1)}, f32[512]{0:T(512)S(1)}) fusion(f32[1024,512]{1,0:T(8,128)S(1)} %get-tuple-element.117, f32[1024,1408]{1,0:T(8,128)} %copy-done.5, f32[1024]{0:T(1024)S(1)} %bitcast.260, f32[1024,512]{1,0:T(8,128)} %get-tuple-element.112, ...), kind=kLoop, calls=%fused_computation.68 | loop fusion | flops 15727616 | bytes 13651968 | tf_op jit(solution)/shard_map/transpose(jvp())/reduce_sum | solution.py:75
  169.9 4.4 %reshape.296 = f32[4,256,8,64]{3,2,1,0:T(8,128)} reshape(f32[1024,512]{1,0:T(8,128)} %get-tuple-element.106) | data formatting | bytes 4194304 | tf_op jit(solution)/shard_map/transpose(jvp())/reshape;transpose(jvp())/reshape | solution.py:62
  174.3 2.8 copy.120
  177.2 2.7 fusion.36
  179.9 1.9 fusion.61
  183.5 1.2 copy-done.4
  184.7 9.8 %fusion.8 = (f32[4,8,256]{2,1,0:T(8,128)}, f32[4,8,256]{2,1,0:T(8,128)}, f32[4,256,256]{2,1,0:T(8,128)S(1)}) fusion(f32[4,256,256]{2,1,0:T(8,128)S(1)} %copy-done.26, f32[4,8,256]{2,1,0:T(8,128)S(1)} %fusion.101, pred[256,256]{1,0:T(8,128)(4,1)S(1)} %copy-done.34, f32[4,256,8,64]{1,3,2,0:T(8,128)S(1)} %copy-done.4, f32[4,8,256]{2,1,0:T(8,128)S(1)} %bitcast.245, ...), kind=kOutput, calls=%fused_computation.10 | convolution fusion | flops 828620800 | bytes 6488064 | tf_op jit(solution)/shard_map/transpose(jvp(chij,chjp->chip))/dot_general | solution.py:51
  194.5 4.4 %fusion.2 = f32[4,8,256,64]{2,3,1,0:T(8,128)S(1)} fusion(f32[4,256,256]{2,1,0:T(8,128)S(1)} %copy-done.26, f32[4,8,256]{2,1,0:T(8,128)S(1)} %fusion.101, pred[256,256]{1,0:T(8,128)(4,1)S(1)} %copy-done.34, f32[4,256,8,64]{1,3,2,0:T(8,128)S(1)} %copy.120), kind=kOutput, calls=%fused_computation.5 | convolution fusion | flops 813694976 | bytes 5341184 | tf_op jit(solution)/shard_map/transpose(jvp(chij,chjp->chip))/dot_general | solution.py:51
  198.9 1.9 fusion.58
  200.8 2.9 fusion.32
  203.7 1.9 convolution_add_fusion
  207.5 1.5 fusion.133
  209.0 2.7 fusion.37
  211.8 2.8 copy.140
  214.6 4.9 %reshape.295 = f32[1024,512]{1,0:T(8,128)} reshape(f32[4,256,8,64]{3,2,1,0:T(8,128)} %copy.140) | data formatting | bytes 4194304 | tf_op jit(solution)/shard_map/transpose(jvp())/reshape | solution.py:37
  219.6 6.0 %multiply_reduce_fusion.5 = (f32[512]{0:T(512)S(1)}, f32[512]{0:T(512)S(1)}, f32[512]{0:T(512)S(1)}, f32[512]{0:T(512)S(1)}, f32[512]{0:T(512)S(1)}, /*index=5*/f32[1024,512]{1,0:T(8,128)S(1)}) fusion(f32[1024,1408]{1,0:T(8,128)} %copy-done.5, f32[1024,512]{1,0:T(8,128)} %slice.215, f32[1024,512]{1,0:T(8,128)S(1)} %copy-done.2, f32[1024,512]{1,0:T(8,128)} %reshape.295, ...), kind=kLoop, calls=%fused_computation.72 | loop fusion | flops 10483200 | bytes 12595200 | tf_op jit(solution)/shard_map/transpose(jvp())/reduce_sum | solution.py:26
  225.6 2.1 multiply_reduce_fusion.11
  228.5 1.3 broadcast_multiply_fusion
  232.9 4.6 %fusion.51 = bf16[1024,1024]{1,0:T(8,128)(2,1)} fusion(bf16[1024,1920]{0,1:T(8,128)(2,1)S(1)} %copy-done.78, bf16[1024,8]{1,0:T(8,128)(2,1)S(1)} %get-tuple-element.108, bf16[1024,256]{1,0:T(8,128)(2,1)S(1)} %fusion.74, bf16[1024,512]{1,0:T(8,128)(2,1)S(1)} %fusion.31, bf16[1024,512]{1,0:T(8,128)(2,1)S(1)} %copy-done.22), kind=kOutput, calls=%fused_computation.91 | convolution fusion | flops 2968256512 | bytes 7864320 | tf_op jit(solution)/shard_map/dot_general | solution.py:86
  237.6 1.5 copy-done.18
  239.1 3.8 %convolution_convert_fusion.1 = bf16[1024,1024]{1,0:T(8,128)(2,1)} fusion(bf16[1024,1920]{0,1:T(8,128)(2,1)} %all-gather.6.cloned.1.call-done, f32[1024,512]{1,0:T(8,128)S(1)} %copy-done.18, f32[1024]{0:T(1024)S(1)} %bitcast.250, f32[512]{0:T(512)S(1)} %copy-done.70), kind=kOutput, calls=%fused_computation.92 | convolution fusion | flops 1076363264 | bytes 5249024 | tf_op jit(solution)/shard_map/dot_general | solution.py:86
  243.0 3.9 %fusion.56 = bf16[1024,512]{0,1:T(8,128)(2,1)} fusion(bf16[1024,1024]{1,0:T(8,128)(2,1)} %all-gather.8.cloned.1.call-done, f32[1024,512]{1,0:T(8,128)S(1)} %copy-done.18, f32[1024]{0:T(1024)S(1)} %bitcast.251, f32[512]{0:T(512)S(1)} %copy-done.70), kind=kOutput, calls=%fused_computation.98 | convolution fusion | flops 1075838976 | bytes 5249024 | tf_op jit(solution)/shard_map/dot_general | solution.py:80
  246.9 1.8 copy.128
  249.7 5.4 %convolution_convert_fusion = bf16[1024,1408]{1,0:T(8,128)(2,1)S(1)} fusion(bf16[1024,1024]{1,0:T(8,128)(2,1)} %all-gather.4.cloned.1.call-done, bf16[1024,8]{1,0:T(8,128)(2,1)S(1)} %get-tuple-element.108, bf16[1024,256]{1,0:T(8,128)(2,1)S(1)} %fusion.74, bf16[1024,512]{1,0:T(8,128)(2,1)} %copy-done.24, bf16[1024,512]{1,0:T(8,128)(2,1)S(1)} %copy-done.23), kind=kOutput, calls=%fused_computation.24 | convolution fusion | flops 2968649728 | bytes 7618560 | tf_op jit(solution)/shard_map/dot_general | solution.py:80
  255.2 2.4 pad_maximum_fusion.p_ref
  257.5 21.4 %reduce-scatter.5.cloned.1.call-done = bf16[256,1024]{1,0:T(8,128)(2,1)} async-done(((bf16[1024,1024]{1,0:T(8,128)(2,1)}), bf16[256,1024]{1,0:T(8,128)(2,1)}) %reduce-scatter.5.cloned.1.call-update) | async-done | bytes 524304 | tf_op jit(solution)/shard_map/reduce_scatter | solution.py:337
  279.0 1.4 fusion.73
  280.4 2.1 copy-done
  282.5 44.3 %shard_map.211 = (f32[128,1920]{1,0:T(8,128)S(1)}, f32[56,128]{1,0:T(8,128)S(1)}) custom-call(bf16[8,128,1920]{2,1,0:T(8,128)(2,1)S(1)} %copy-done, f32[56,128]{1,0:T(8,128)S(1)} %pad_maximum_fusion.4.small_ref), custom_call_target="tpu_custom_call" | custom-call | tf_op jit(solution)/shard_map/pallas_call | solution.py:241
  332.9 2.8 fusion.63
  (232 shorter events, 22.6 us)
Async XLA Ops:
  7.2 4.2 %copy-start.32 = (bf16[128,256]{1,0:T(8,128)(2,1)S(1)}, bf16[128,256]{1,0:T(8,128)(2,1)}, u32[]{:S(2)}) copy-start(bf16[128,256]{1,0:T(8,128)(2,1)} %param.17) | copy-start | bytes 196612
  7.2 4.3 %copy-start.29 = (bf16[128,512]{1,0:T(8,128)(2,1)S(1)}, bf16[128,512]{1,0:T(8,128)(2,1)}, u32[]{:S(2)}) copy-start(bf16[128,512]{1,0:T(8,128)(2,1)} %param.15) | copy-start | bytes 393220
  7.2 4.5 %copy-start.30 = (bf16[128,512]{1,0:T(8,128)(2,1)S(1)}, bf16[128,512]{1,0:T(8,128)(2,1)}, u32[]{:S(2)}) copy-start(bf16[128,512]{1,0:T(8,128)(2,1)} %param.16) | copy-start | bytes 393220
  7.2 4.7 %copy-start.75 = (bf16[128,8]{0,1:T(8,128)(2,1)S(1)}, bf16[128,8]{0,1:T(8,128)(2,1)}, u32[]{:S(2)}) copy-start(bf16[128,8]{0,1:T(8,128)(2,1)} %param.18) | copy-start | bytes 6148
  7.2 4.7 %copy-start.31 = (bf16[512,128]{1,0:T(8,128)(2,1)S(1)}, bf16[512,128]{1,0:T(8,128)(2,1)}, u32[]{:S(2)}) copy-start(bf16[512,128]{1,0:T(8,128)(2,1)} %param.23) | copy-start | bytes 393220
  7.2 52.9 %all-gather.4.cloned.1.call-start = ((), (), s32[]{:S(2)}) async-start(), calls=%async_computation.2 | async-start | bytes 2621440 | tf_op jit(solution)/shard_map/all_gather | solution.py:294
  9.2 4.9 %copy-start.76 = (f32[3,8]{1,0:T(4,128)S(1)}, f32[3,8]{1,0:T(4,128)}, u32[]{:S(2)}) copy-start(f32[3,8]{1,0:T(4,128)} %param.21) | copy-start | bytes 292
  9.2 5.1 %copy-start.68 = (f32[5,256]{1,0:T(8,128)S(1)}, f32[5,256]{1,0:T(8,128)}, u32[]{:S(2)}) copy-start(f32[5,256]{1,0:T(8,128)} %param.20) | copy-start | bytes 15364
  9.2 5.1 %copy-start.62 = (f32[5,512]{1,0:T(8,128)S(1)}, f32[5,512]{1,0:T(8,128)}, u32[]{:S(2)}) copy-start(f32[5,512]{1,0:T(8,128)} %param.19) | copy-start | bytes 30724
  11.3 86.3 %all-gather.6.cloned.1.call-start = ((), (), s32[]{:S(2)}) async-start(), calls=%async_computation.3 | async-start | bytes 4423680 | tf_op jit(solution)/shard_map/all_gather | solution.py:300
  12.7 132.4 %all-gather.8.cloned.1.call-start = ((), (), s32[]{:S(2)}) async-start(), calls=%async_computation.4 | async-start | bytes 2621440 | tf_op jit(solution)/shard_map/all_gather | solution.py:301
  13.5 265.5 %reduce-scatter.5.cloned.1.call-start = ((), (), s32[]{:S(2)}) async-start(), calls=%async_computation.6 | async-start | bytes 2621440 | tf_op jit(solution)/shard_map/reduce_scatter | solution.py:337
  14.2 91.3 %copy-start.65 = (f32[8]{0:T(128)}, f32[8]{0:T(128)S(1)}, u32[]{:S(2)}) copy-start(f32[8]{0:T(128)S(1)} %get-tuple-element.156) | copy-start | bytes 100
  14.2 99.2 %copy-start.73 = (f32[8]{0:T(128)}, f32[8]{0:T(128)S(1)}, u32[]{:S(2)}) copy-start(f32[8]{0:T(128)S(1)} %get-tuple-element.157) | copy-start | bytes 100
  14.4 130.8 %copy-start.46 = (f32[512]{0:T(512)}, f32[512]{0:T(512)S(1)}, u32[]{:S(2)}) copy-start(f32[512]{0:T(512)S(1)} %mul.618) | copy-start | bytes 6148
  14.4 108.1 %copy-start.50 = (f32[1,256]{1,0:T(1,128)}, f32[1,256]{1,0:T(1,128)S(1)}, u32[]{:S(2)}) copy-start(f32[1,256]{1,0:T(1,128)S(1)} %get-tuple-element.151) | copy-start | bytes 3076
  14.4 108.1 %copy-start.52 = (f32[1,256]{1,0:T(1,128)}, f32[1,256]{1,0:T(1,128)S(1)}, u32[]{:S(2)}) copy-start(f32[1,256]{1,0:T(1,128)S(1)} %get-tuple-element.152) | copy-start | bytes 3076
  14.4 108.1 %copy-start.54 = (f32[1,256]{1,0:T(1,128)}, f32[1,256]{1,0:T(1,128)S(1)}, u32[]{:S(2)}) copy-start(f32[1,256]{1,0:T(1,128)S(1)} %get-tuple-element.153) | copy-start | bytes 3076
  14.4 108.1 %copy-start.56 = (f32[1,256]{1,0:T(1,128)}, f32[1,256]{1,0:T(1,128)S(1)}, u32[]{:S(2)}) copy-start(f32[1,256]{1,0:T(1,128)S(1)} %get-tuple-element.154) | copy-start | bytes 3076
  14.4 92.7 %copy-start.38 = (f32[1,512]{1,0:T(1,128)}, f32[1,512]{1,0:T(1,128)S(1)}, u32[]{:S(2)}) copy-start(f32[1,512]{1,0:T(1,128)S(1)} %get-tuple-element.144) | copy-start | bytes 6148
  14.4 92.7 %copy-start.40 = (f32[1,512]{1,0:T(1,128)}, f32[1,512]{1,0:T(1,128)S(1)}, u32[]{:S(2)}) copy-start(f32[1,512]{1,0:T(1,128)S(1)} %get-tuple-element.145) | copy-start | bytes 6148
  14.5 92.7 %copy-start.42 = (f32[1,512]{1,0:T(1,128)}, f32[1,512]{1,0:T(1,128)S(1)}, u32[]{:S(2)}) copy-start(f32[1,512]{1,0:T(1,128)S(1)} %get-tuple-element.146) | copy-start | bytes 6148
  14.5 92.7 %copy-start.44 = (f32[1,512]{1,0:T(1,128)}, f32[1,512]{1,0:T(1,128)S(1)}, u32[]{:S(2)}) copy-start(f32[1,512]{1,0:T(1,128)S(1)} %get-tuple-element.147) | copy-start | bytes 6148
  14.5 111.6 %copy-start.71 = (f32[4]{0:T(128)}, f32[4]{0:T(128)S(1)}, u32[]{:S(2)}) copy-start(f32[4]{0:T(128)S(1)} %pad.182.clone) | copy-start | bytes 52
  103.5 3.2 copy-start.5
  103.6 19.0 %copy-start.6 = (f32[1024,256]{1,0:T(8,128)}, f32[1024,256]{1,0:T(8,128)S(1)}, u32[]{:S(2)}) copy-start(f32[1024,256]{1,0:T(8,128)S(1)} %slice.212) | copy-start | bytes 3145732
  113.4 50.4 %copy-start.1 = (f32[1024,512]{1,0:T(8,128)}, f32[1024,512]{1,0:T(8,128)S(1)}, u32[]{:S(2)}) copy-start(f32[1024,512]{1,0:T(8,128)S(1)} %get-tuple-element.117) | copy-start | bytes 6291460
  122.4 2.9 copy-start.58
  122.4 2.9 copy-start.60
  122.4 2.9 copy-start.63
  139.2 5.9 %copy-start.69 = (f32[512]{0:T(512)S(1)}, f32[512]{0:T(512)}, u32[]{:S(2)}) copy-start(f32[512]{0:T(512)} %param.22) | copy-start | bytes 6148
  177.2 2.7 copy-start.15
  177.2 2.7 copy-start.17
  198.9 4.8 %copy-start.9 = (f32[4,8,256,64]{2,3,1,0:T(8,128)}, f32[4,8,256,64]{2,3,1,0:T(8,128)S(1)}, u32[]{:S(2)}) copy-start(f32[4,8,256,64]{2,3,1,0:T(8,128)S(1)} %fusion.2) | copy-start | bytes 6291460
  214.6 4.9 %copy-start.2 = (f32[1024,512]{1,0:T(8,128)S(1)}, f32[1024,512]{1,0:T(8,128)}, u32[]{:S(2)}) copy-start(f32[1024,512]{1,0:T(8,128)} %copy-done.1) | copy-start | bytes 6291460
  214.6 4.9 %copy-start.47 = (f32[512]{0:T(512)S(1)}, f32[512]{0:T(512)}, u32[]{:S(2)}) copy-start(f32[512]{0:T(512)} %copy-done.46) | copy-start | bytes 6148
  219.5 6.0 %copy-start.7 = (f32[1024,256]{1,0:T(8,128)S(1)}, f32[1024,256]{1,0:T(8,128)}, u32[]{:S(2)}) copy-start(f32[1024,256]{1,0:T(8,128)} %copy-done.6) | copy-start | bytes 3145732
  219.5 6.0 %copy-start.13 = (f32[1024,256]{1,0:T(8,128)S(1)}, f32[1024,256]{1,0:T(8,128)}, u32[]{:S(2)}) copy-start(f32[1024,256]{1,0:T(8,128)} %get-tuple-element.119) | copy-start | bytes 3145732
  219.5 6.0 %copy-start.19 = (f32[4,256,128]{2,1,0:T(8,128)S(1)}, f32[4,256,128]{2,1,0:T(8,128)}, u32[]{:S(2)}) copy-start(f32[4,256,128]{2,1,0:T(8,128)} %convolution_add_fusion) | copy-start | bytes 1572868
  230.1 2.8 copy-start.78
  237.5 95.4 %reduce-scatter.3.cloned.1.call-start = ((), (), s32[]{:S(2)}) async-start(), calls=%async_computation.5 | async-start | bytes 2621440 | tf_op jit(solution)/shard_map/reduce_scatter | solution.py:321
  246.9 2.8 copy-start.23
  255.1 23.8 %copy-start.8 = (bf16[256,1024]{1,0:T(8,128)(2,1)S(1)}, bf16[256,1024]{1,0:T(8,128)(2,1)}, u32[]{:S(2)}) copy-start(bf16[256,1024]{1,0:T(8,128)(2,1)} %param.12) | copy-start | bytes 1572868
  255.1 23.8 %copy-start.35 = (f32[1024]{0:T(1024)S(1)}, f32[1024]{0:T(1024)}, u32[]{:S(2)}) copy-start(f32[1024]{0:T(1024)} %param.14) | copy-start | bytes 12292
  255.2 23.8 %copy-start.49 = (f32[256]{0:T(256)S(1)}, f32[256]{0:T(256)}, u32[]{:S(2)}) copy-start(f32[256]{0:T(256)} %copy-done.48) | copy-start | bytes 3076
  326.9 6.0 %copy-start.20 = (bf16[256,1024]{1,0:T(8,128)(2,1)S(1)}, bf16[256,1024]{1,0:T(8,128)(2,1)}, u32[]{:S(2)}) copy-start(bf16[256,1024]{1,0:T(8,128)(2,1)} %param.13) | copy-start | bytes 1572868
  326.9 6.0 %copy-start.21 = (bf16[256,1024]{1,0:T(8,128)(2,1)S(1)}, bf16[256,1024]{1,0:T(8,128)(2,1)}, u32[]{:S(2)}) copy-start(bf16[256,1024]{1,0:T(8,128)(2,1)} %reduce-scatter.5.cloned.1.call-done) | copy-start | bytes 1572868
  326.9 6.0 %copy-start.67 = (f32[256]{0:T(256)S(1)}, f32[256]{0:T(256)}, u32[]{:S(2)}) copy-start(f32[256]{0:T(256)} %get-tuple-element.161) | copy-start | bytes 3076
  (36 other events, 61.9 us)
Sparse Core Ops, SparseCore 0:
  11.5 48.6 all-gather.3
  62.6 34.9 all-gather.5
  99.2 45.9 all-gather.7
  237.7 41.2 reduce-scatter.4
  281.2 46.4 reduce-scatter.2
